TPU v7x, 128 devices: a whole 4x4x4 slice. The times are simulated.
128 devices in a mesh: gx: 8 (over y_hi, x), yz: 16 (over z, y_lo, core).
Axes of the slice: x: 4, y: 4 (y_hi: 2, y_lo: 2; y = y_hi * 2 + y_lo), z: 4, core: 2. Of those that a mesh axis runs over, the one named last changes fastest.
Arguments:
- decode_rows: bfloat16 [1536, 16384], P('yz', 'gx'), may hold values from -6 to 6
- attended: bfloat16 [1536, 16384], P('yz', 'gx'), may hold values from -6 to 6
- qkv_values: bfloat16 [16384, 18432], P(('gx', 'yz')), may hold values from -6 to 6
- qkv_scales: bfloat16 [128, 144], P(('gx', 'yz')), may hold values from 0.0023345947 to 0.0234375
- out_values: bfloat16 [16384, 16384], P(('gx', 'yz')), may hold values from -6 to 6
- out_scales: bfloat16 [128, 128], P(('gx', 'yz')), may hold values from 0.0023345947 to 0.0234375
Outputs:
- qkv: bfloat16 [1536, 18432], P('gx', 'yz')
- projected: bfloat16 [1536, 16384], P('gx', 'yz')
All inputs are finite; a program needn't handle non-finite values.
Results may differ from a plain program's by a relative error of at most 0.005.
Values may be sent and summed in bfloat16 or wider, within the bound.
A program may use at most 128 MiB of HBM per device.

v0:
```python
import jax
import jax.numpy as jnp
from jax import lax
from jax.sharding import PartitionSpec as P

TILE = 128


def dequantize(values, scales):
    rows, cols = values.shape
    tiled = values.reshape(rows // TILE, TILE, cols // TILE, TILE).astype(jnp.float32)
    scaled = tiled * scales.astype(jnp.float32)[:, None, :, None]
    return scaled.reshape(rows, cols).astype(jnp.bfloat16)


def local(decode_rows, attended, qkv_values, qkv_scales, out_values, out_scales):
    qkv_local, qkv_factor, out_local, out_factor = (
        lax.all_to_all(qkv_values, "yz", split_axis=1, concat_axis=0, tiled=True),
        lax.all_to_all(qkv_scales, "yz", split_axis=1, concat_axis=0, tiled=True),
        lax.all_to_all(out_values, "yz", split_axis=1, concat_axis=0, tiled=True),
        lax.all_to_all(out_scales, "yz", split_axis=1, concat_axis=0, tiled=True),
    )
    qkv_weight = dequantize(qkv_local, qkv_factor)
    out_weight = dequantize(out_local, out_factor)
    all_hidden, all_context = (
        lax.all_gather(decode_rows, "yz", axis=0, tiled=True),
        lax.all_gather(attended, "yz", axis=0, tiled=True),
    )
    qkv_terms = jnp.dot(all_hidden, qkv_weight, preferred_element_type=jnp.float32)
    qkv = lax.psum_scatter(qkv_terms, "gx", scatter_dimension=0, tiled=True).astype(jnp.bfloat16)
    out_terms = jnp.dot(all_context, out_weight, preferred_element_type=jnp.float32)
    projected = lax.psum_scatter(out_terms, "gx", scatter_dimension=0, tiled=True).astype(
        jnp.bfloat16
    )
    return (qkv, projected)


def solution(mesh):
    in_specs = (
        P("yz", "gx"),
        P("yz", "gx"),
        P(("gx", "yz"), None),
        P(("gx", "yz"), None),
        P(("gx", "yz"), None),
        P(("gx", "yz"), None),
    )
    out_specs = (P("gx", "yz"), P("gx", "yz"))
    return jax.shard_map(local, mesh=mesh, in_specs=in_specs, out_specs=out_specs, check_vma=False)
```

profile of v0, /device:TPU:1, one launch (start us, length us, event | category | flops | bytes accessed | tf_op | source)
XLA Modules:
  0.0 413.0 jit_solution(9203193080526350363)
XLA Ops:
  7.2 0.7 all-gather.5.cloned.1.call-update
  7.9 0.7 all-gather.3.cloned.1.call-update
  9.2 1.3 reduce.4
  10.5 0.7 all_to_all.49
  11.2 7.8 %all-to-all-start.3 = ((bf16[1,16,8]{2,0,1:T(2,128)(2,1)}), bf16[1,16,8]{2,0,1:T(2,128)(2,1)S(1)}, u32[]{:S(2)}, u32[]{:S(2)}) async-start(bf16[1,16,8]{2,0,1:T(2,128)(2,1)} %all_to_all.49), calls=%async_computation.3 | async-start | bytes 16384 | tf_op jit(solution)/shard_map/all_to_all | solution.py:21
  19.0 6.4 %copy.44 = bf16[128,16384]{0,1:T(8,128)(2,1)} copy(bf16[128,16384]{1,0:T(8,128)(2,1)} %param.10) | data formatting | bytes 8388608 | tf_op args[4]
  25.4 5.7 %all-to-all-start.2 = ((bf16[128,16,1024]{0,2,1:T(8,128)(2,1)}), bf16[128,16,1024]{0,2,1:T(8,128)(2,1)}, u32[]{:S(2)}, u32[]{:S(2)}) async-start(bf16[128,16,1024]{0,2,1:T(8,128)(2,1)} %bitcast.43), calls=%async_computation.2 | async-start | bytes 8388608 | tf_op jit(solution)/shard_map/all_to_all | solution.py:20
  31.3 75.3 %all-to-all-done.2 = bf16[128,16,1024]{0,2,1:T(8,128)(2,1)} async-done(((bf16[128,16,1024]{0,2,1:T(8,128)(2,1)}), bf16[128,16,1024]{0,2,1:T(8,128)(2,1)}, u32[]{:S(2)}, u32[]{:S(2)}) %all-to-all-start.2) | async-done | bytes 4194336 | tf_op jit(solution)/shard_map/all_to_all | solution.py:20
  106.6 6.3 %convert_bitcast_fusion.1 = f32[16,128,1024]{1,2,0:T(8,128)} fusion(bf16[128,16,1024]{0,2,1:T(8,128)(2,1)} %all-to-all-done.2), kind=kLoop, calls=%fused_computation.7 | loop fusion | flops 2097152 | bytes 12582912 | tf_op jit(solution)/shard_map/convert_element_type | solution.py:11
  112.9 9.4 %copy.45 = f32[16,128,1024]{2,1,0:T(8,128)} copy(f32[16,128,1024]{1,2,0:T(8,128)} %convert_bitcast_fusion.1) | data formatting | bytes 16777216 | tf_op jit(solution)/shard_map/convert_element_type | solution.py:11
  122.3 3.8 mul.25
  126.1 9.8 %fusion.1 = bf16[2048,1024]{1,0:T(8,128)(2,1)} fusion(f32[256,8,8,128]{3,2,1,0:T(8,128)} %bitcast.41, f32[16,128,1024]{2,1,0:T(8,128)} %copy.45), kind=kLoop, calls=%fused_computation.6 | loop fusion | flops 4194304 | bytes 20971520 | tf_op jit(solution)/shard_map/convert_element_type | solution.py:13
  135.9 12.1 %convolution_bitcast_fusion.1 = f32[1536,1024]{0,1:T(8,128)} fusion(bf16[2048,1024]{1,0:T(8,128)(2,1)} %fusion.1, bf16[1536,2048]{1,0:T(8,128)(2,1)} %all-gather.5.cloned.1.call-done), kind=kOutput, calls=%fused_computation.8 | convolution fusion | flops 6442450944 | bytes 16777216 | tf_op jit(solution)/shard_map/dot_general | solution.py:31
  148.0 6.5 %copy.53 = f32[1536,1024]{1,0:T(8,128)} copy(f32[1536,1024]{0,1:T(8,128)} %convolution_bitcast_fusion.1) | data formatting | bytes 12582912
  155.2 0.7 all_to_all.48
  155.9 4.0 all-to-all-start.1
  159.9 6.7 %copy.39 = bf16[128,18432]{0,1:T(8,128)(2,1)} copy(bf16[128,18432]{1,0:T(8,128)(2,1)} %param.8) | data formatting | bytes 9437184 | tf_op args[2]
  166.6 5.8 %all-to-all-start = ((bf16[128,16,1152]{0,2,1:T(8,128)(2,1)}), bf16[128,16,1152]{0,2,1:T(8,128)(2,1)}, u32[]{:S(2)}, u32[]{:S(2)}) async-start(bf16[128,16,1152]{0,2,1:T(8,128)(2,1)} %bitcast.42), calls=%async_computation | async-start | bytes 9437184 | tf_op jit(solution)/shard_map/all_to_all | solution.py:18
  172.7 0.7 mul.22
  173.4 8.3 %copy.59 = f32[144,8,16,128]{3,1,2,0:T(8,128)} copy(f32[144,8,16,128]{3,2,1,0:T(8,128)S(1)} %bitcast.39) | data formatting | bytes 18874368
  181.7 9.7 %copy.43 = f32[2048,1152]{1,0:T(8,128)} copy(f32[2048,1152]{0,1:T(8,128)} %bitcast.40) | data formatting | bytes 18874368 | tf_op jit(solution)/shard_map/mul | solution.py:12
  191.4 61.8 %all-to-all-done = bf16[128,16,1152]{0,2,1:T(8,128)(2,1)} async-done(((bf16[128,16,1152]{0,2,1:T(8,128)(2,1)}), bf16[128,16,1152]{0,2,1:T(8,128)(2,1)}, u32[]{:S(2)}, u32[]{:S(2)}) %all-to-all-start) | async-done | bytes 4718624 | tf_op jit(solution)/shard_map/all_to_all | solution.py:18
  253.2 7.0 %convert_bitcast_fusion = f32[16,128,1152]{1,2,0:T(8,128)} fusion(bf16[128,16,1152]{0,2,1:T(8,128)(2,1)} %all-to-all-done), kind=kLoop, calls=%fused_computation.3 | loop fusion | flops 2359296 | bytes 14155776 | tf_op jit(solution)/shard_map/convert_element_type | solution.py:11
  260.2 10.0 %copy.40 = f32[16,128,1152]{2,1,0:T(8,128)} copy(f32[16,128,1152]{1,2,0:T(8,128)} %convert_bitcast_fusion) | data formatting | bytes 18874368 | tf_op jit(solution)/shard_map/convert_element_type | solution.py:11
  270.1 9.7 %fusion = bf16[2048,1152]{1,0:T(8,128)(2,1)} fusion(f32[2048,1152]{1,0:T(8,128)} %copy.43, f32[16,128,1152]{2,1,0:T(8,128)} %copy.40), kind=kLoop, calls=%fused_computation.2 | loop fusion | flops 4718592 | bytes 23592960 | tf_op jit(solution)/shard_map/convert_element_type | solution.py:13
  279.9 13.0 %convolution_bitcast_fusion = f32[1536,1152]{0,1:T(8,128)} fusion(bf16[2048,1152]{1,0:T(8,128)(2,1)} %fusion, bf16[1536,2048]{1,0:T(8,128)(2,1)} %all-gather.3.cloned.1.call-done), kind=kOutput, calls=%fused_computation.4 | convolution fusion | flops 7247757312 | bytes 18087936 | tf_op jit(solution)/shard_map/dot_general | solution.py:29
  292.9 8.0 %copy.51 = f32[1536,1152]{1,0:T(8,128)} copy(f32[1536,1152]{0,1:T(8,128)} %convolution_bitcast_fusion) | data formatting | bytes 14155776
  301.0 1.3 copy.54
  302.3 0.9 copy.50
  303.3 100.8 %reduce-scatter.7.cloned.1.call-done = f32[192,1152]{1,0:T(8,128)} async-done(((f32[1536,1152]{1,0:T(8,128)}), f32[192,1152]{1,0:T(8,128)}) %reduce-scatter.7.cloned.1.call-update) | async-done | bytes 884752
  404.0 1.4 copy.52
  405.5 1.0 copy.49
  (20 shorter events, 1.8 us)
Async XLA Ops:
  7.2 128.7 %all-gather.5.cloned.1.call-start = ((), (), s32[]{:S(2)}) async-start(), calls=%async_computation.7 | async-start | bytes 6684672 | tf_op jit(solution)/shard_map/all_gather | solution.py:27
  7.9 272.0 %all-gather.3.cloned.1.call-start = ((), (), s32[]{:S(2)}) async-start(), calls=%async_computation.6 | async-start | bytes 6684672 | tf_op jit(solution)/shard_map/all_gather | solution.py:26
  11.2 14.2 %all-to-all-start.3 = ((bf16[1,16,8]{2,0,1:T(2,128)(2,1)}), bf16[1,16,8]{2,0,1:T(2,128)(2,1)S(1)}, u32[]{:S(2)}, u32[]{:S(2)}) async-start(bf16[1,16,8]{2,0,1:T(2,128)(2,1)} %all_to_all.49), calls=%async_computation.3 | async-start | bytes 16384 | tf_op jit(solution)/shard_map/all_to_all | solution.py:21
  25.4 81.2 %all-to-all-start.2 = ((bf16[128,16,1024]{0,2,1:T(8,128)(2,1)}), bf16[128,16,1024]{0,2,1:T(8,128)(2,1)}, u32[]{:S(2)}, u32[]{:S(2)}) async-start(bf16[128,16,1024]{0,2,1:T(8,128)(2,1)} %bitcast.43), calls=%async_computation.2 | async-start | bytes 8388608 | tf_op jit(solution)/shard_map/all_to_all | solution.py:20
  31.1 269.9 %reduce-scatter.9.cloned.1.call-start = ((), (), s32[]{:S(2)}) async-start(), calls=%async_computation.9 | async-start | bytes 7077888
  154.5 0.7 copy-start
  155.9 10.6 %all-to-all-start.1 = ((bf16[1,16,9]{2,0,1:T(2,128)(2,1)}), bf16[1,16,9]{2,0,1:T(2,128)(2,1)S(1)}, u32[]{:S(2)}, u32[]{:S(2)}) async-start(bf16[1,16,9]{2,0,1:T(2,128)(2,1)} %all_to_all.48), calls=%async_computation.1 | async-start | bytes 16384 | tf_op jit(solution)/shard_map/all_to_all | solution.py:19
  166.6 86.6 %all-to-all-start = ((bf16[128,16,1152]{0,2,1:T(8,128)(2,1)}), bf16[128,16,1152]{0,2,1:T(8,128)(2,1)}, u32[]{:S(2)}, u32[]{:S(2)}) async-start(bf16[128,16,1152]{0,2,1:T(8,128)(2,1)} %bitcast.42), calls=%async_computation | async-start | bytes 9437184 | tf_op jit(solution)/shard_map/all_to_all | solution.py:18
  172.4 231.7 %reduce-scatter.7.cloned.1.call-start = ((), (), s32[]{:S(2)}) async-start(), calls=%async_computation.8 | async-start | bytes 7962624
Sparse Core Ops, SparseCore 0:
  9.7 93.1 all-gather.4
  104.6 42.7 all-gather.2
  154.7 127.2 reduce-scatter.8
  301.1 102.9 reduce-scatter.6
where the time goes:
time: 414 us; the launch traced here: 413 us
  waiting for transfers between devices  239 us (58%)
  local copies, waits for them, and re-layouts  77 us (19%)
  other arithmetic  34.1 us (8%)
  matrix products  25.1 us (6%)
  starting transfers between devices  23.7 us (6%)
  between operations  13.8 us (3%)
    unnamed x6, waiting for transfers between devices  102 us
    all_to_all x1, waiting for transfers between devices, local(): lax.all_to_all(out_values, 'yz', split_axis=1, concat_axis=0, tiled=True)  75.3 us
    all_to_all x1, waiting for transfers between devices, local(): lax.all_to_all(qkv_values, 'yz', split_axis=1, concat_axis=0, tiled=True)  61.8 us
    unnamed x12, local copies, waits for them, and re-layouts  41.7 us
    convert_element_type x2, other arithmetic, dequantize(): return scaled.reshape(rows, cols).astype(jnp.bfloat16)  19.5 us
    convert_element_type x2, local copies, waits for them, and re-layouts, dequantize(): values.reshape(rows // TILE, TILE, cols // TILE, TILE).astype(jnp.float32)  19.4 us
    mul x3, local copies, waits for them, and re-layouts, dequantize(): scaled = tiled * scales.astype(jnp.float32)[:, None, :, None]  14.2 us
    convert_element_type x2, other arithmetic, dequantize(): values.reshape(rows // TILE, TILE, cols // TILE, TILE).astype(jnp.float32)  13.3 us
  transfers between devices with their start and end apart: 8, of which 3 were waited for; matrix products, arithmetic and copies ran while one was open for 32% of the time, Pallas kernels for 0%

commit v1 on v0

v1 whole, which is shorter than its diff:
```python
import jax
import jax.numpy as jnp
from jax import lax
from jax.experimental import pallas as pl
from jax.experimental.pallas import tpu as pltpu
from jax.sharding import PartitionSpec as P

MESH = pl.DeviceIdType.MESH
F32 = jnp.float32
BF16 = jnp.bfloat16

QCH, QW = 9, 256
OCH, OW = 4, 512
STEPS = (
    ("q", 0), ("o", 0), ("q", 1), ("q", 2), ("o", 1), ("q", 3), ("q", 4),
    ("o", 2), ("q", 5), ("q", 6), ("o", 3), ("q", 7), ("q", 8),
)


def kernel(
    rows_q, rows_o, val_q, val_o, sc_q, sc_o,
    out_q, out_o,
    in_q, in_o, x_q, x_o, a_q, a_o, snd_q, snd_o, w_q, w_o, p_q, p_o,
    far_q, far_o, rx_q, rx_o, ph_q, ph_o, swap,
    ld, s1s, s1q, s1o, s2s, s2q, s2o, sbs, sbq, sbo,
    wsq, wso, wrq, wro, fsq, fso, frq, fro, rsq, rso, rrq, rro, psq, pso, prq, pro, sws, swr,
):
    g = lax.axis_index("gx")
    w = lax.axis_index("yz")
    x, yh = lax.rem(g, 4), lax.div(g, 4)
    c, yl, z = lax.rem(w, 2), lax.rem(lax.div(w, 2), 2), lax.div(w, 4)
    y = yh * 2 + yl

    def dev(dx=0, dy=0, dz=0, dc=0):
        xx, yy, zz, cc = (lax.rem(x + dx, 4), lax.rem(y + dy, 4), lax.rem(z + dz, 4), lax.rem(c + dc, 2))
        return (lax.div(yy, 2) * 4 + xx, zz * 4 + lax.rem(yy, 2) * 2 + cc)

    mate = (g, z * 4 + (1 - yl) * 2 + c)
    sib = dev(dc=1)

    def remote(src, dst, ssem, rsem, to):
        return pltpu.make_async_remote_copy(
            src_ref=src, dst_ref=dst, send_sem=ssem, recv_sem=rsem, device_id=to, device_id_type=MESH
        )

    def drain(ref, sem):
        pltpu.make_async_copy(ref, ref, sem).wait()

    loads = []
    for half in range(2):
        for zz in range(4):
            loads.append(pltpu.make_async_copy(
                rows_q.at[:, pl.ds(zz * 512 + half * 256, 256)],
                x_q.at[half, :, pl.ds(zz * 256, 256)], ld.at[0]))
    for zz in range(4):
        loads.append(pltpu.make_async_copy(
            rows_o.at[:, pl.ds(zz * 512, 512)], x_o.at[zz], ld.at[1]))
    loads.append(pltpu.make_async_copy(val_q, in_q, ld.at[2]))
    loads.append(pltpu.make_async_copy(val_o, in_o, ld.at[3]))
    for cp in loads:
        cp.start()

    peers = [dev(dy=dy, dz=dz) for dy in range(4) for dz in range(4) if (dy, dz) != (0, 0)]
    peers += [dev(dz=dz, dc=1) for dz in range(4)]
    peers += [dev(dy=dy, dc=1) for dy in range(1, 4)]
    peers += [dev(dx=1), dev(dx=3)]
    barrier = pltpu.get_barrier_semaphore()
    for peer in peers:
        pl.semaphore_signal(barrier, inc=1, device_id=peer, device_id_type=MESH)
    pl.semaphore_wait(barrier, len(peers))

    own_cols = pl.ds(pl.multiple_of(yh * 512, 512), 512)
    drain(x_q, ld.at[0])
    drain(x_o, ld.at[1])
    q1 = remote(x_q.at[1 - yl], a_q.at[z, yl, c], s1s.at[0], s1q.at[0], mate)
    q1.start()
    o1 = []
    for k in (2, 1, 3):
        cp = remote(x_o.at[lax.rem(z + k, 4)], a_o.at[z, yl, c, :, own_cols], s1s.at[k], s1o.at[k], dev(dz=k))
        cp.start()
        o1.append(cp)
    q1l = pltpu.make_async_copy(x_q.at[yl], a_q.at[z, yl, c], s1q.at[1])
    q1l.start()
    o1l = pltpu.make_async_copy(x_o.at[z], a_o.at[z, yl, c, :, own_cols], s1o.at[0])
    o1l.start()

    def weights_q(ch):
        @pl.loop(0, 8)
        def _(d):
            for half in range(2):
                block = lax.div(d, 2) * 4 + half * 2 + lax.rem(d, 2)
                col = pl.multiple_of(block * 1152 + ch * 128, 128)
                s = sc_q[0, block * 9 + ch]
                snd_q[ch, d, :, half * 128:(half + 1) * 128] = (
                    in_q[:, pl.ds(col, 128)].astype(F32) * s).astype(BF16)
        here = pl.ds(pl.multiple_of((z * 2 + c) * 128, 128), 128)
        for k, dc in ((2, 0), (2, 1), (1, 0), (3, 0), (1, 1), (3, 1), (0, 1)):
            slot = lax.rem(z + k, 4) * 2 + lax.rem(c + dc, 2)
            remote(snd_q.at[ch, slot], w_q.at[ch, here], wsq.at[ch], wrq.at[ch], dev(dz=k, dc=dc)).start()
        pltpu.make_async_copy(snd_q.at[ch, z * 2 + c], w_q.at[ch, here], wrq.at[ch]).start()

    def weights_o(ch):
        @pl.loop(0, 8)
        def _(d):
            for zz in range(4):
                block = zz * 4 + lax.rem(d, 4)
                tile = block * 8 + lax.div(d, 4) * 4 + ch
                col = pl.multiple_of(tile * 128, 128)
                s = sc_o[0, tile]
                snd_o[ch, d, :, zz * 128:(zz + 1) * 128] = (
                    in_o[:, pl.ds(col, 128)].astype(F32) * s).astype(BF16)
        here = pl.ds(pl.multiple_of((y * 2 + c) * 128, 128), 128)
        for k, dc in ((2, 0), (2, 1), (1, 0), (3, 0), (1, 1), (3, 1), (0, 1)):
            slot = lax.rem(y + k, 4) * 2 + lax.rem(c + dc, 2)
            remote(snd_o.at[ch, slot], w_o.at[ch, here], wso.at[ch], wro.at[ch], dev(dy=k, dc=dc)).start()
        pltpu.make_async_copy(snd_o.at[ch, y * 2 + c], w_o.at[ch, here], wro.at[ch]).start()

    drain(in_q, ld.at[2])
    weights_q(0)

    q1.wait_recv()
    q1l.wait()
    q2 = []
    mine = a_q.at[z, :, c]
    for k in (2, 1, 3):
        cp = remote(mine, mine, s2s.at[k], s2q.at[k], dev(dz=k))
        cp.start()
        q2.append((k, cp))
    sibs = [remote(mine, mine, sbs.at[0], sbq.at[0], sib)]
    sibs[0].start()
    for cp in o1:
        cp.wait_recv()
    o1l.wait()
    o2 = []
    mine = a_o.at[:, yl, c, :, own_cols]
    for k in (2, 1, 3):
        cp = remote(mine, mine, s2s.at[4 + k], s2o.at[k], dev(dy=k))
        cp.start()
        o2.append((k, cp))
    sibs.append(remote(mine, mine, sbs.at[4], sbo.at[0], sib))
    sibs[-1].start()

    drain(in_o, ld.at[3])
    for p, ch in STEPS[1:]:
        (weights_q if p == "q" else weights_o)(ch)

    for k, cp in q2:
        cp.wait_recv()
        part = a_q.at[lax.rem(z + 4 - k, 4), :, c]
        fw = remote(part, part, sbs.at[k], sbq.at[k], sib)
        fw.start()
        sibs.append(fw)
    for k, cp in o2:
        cp.wait_recv()
        yy = lax.rem(y + 4 - k, 4)
        part = a_o.at[:, lax.rem(yy, 2), c, :, pl.ds(pl.multiple_of(lax.div(yy, 2) * 512, 512), 512)]
        fw = remote(part, part, sbs.at[4 + k], sbo.at[k], sib)
        fw.start()
        sibs.append(fw)
    for cp in sibs:
        cp.wait_recv()

    right, left = dev(dx=1), dev(dx=3)
    xr, xl, xo = lax.rem(x + 1, 4), lax.rem(x + 3, 4), lax.rem(x + 2, 4)
    refs = {
        "q": (a_q, w_q, p_q, far_q, rx_q, wrq, fsq, frq, rsq, rrq),
        "o": (a_o, w_o, p_o, far_o, rx_o, wro, fso, fro, rso, rro),
    }
    width = {"q": QW, "o": OW}

    def compute(p, ch):
        a, wt, part, far, rx, wr, fs, fr, rs, rr = refs[p]
        drain(wt.at[ch], wr.at[ch])

        @pl.loop(0, 4)
        def _(i):
            lhs = a[i].reshape(384, 1024)
            acc = jnp.dot(lhs, wt[ch], preferred_element_type=F32)
            part[ch, lax.div(i, 2), pl.ds(lax.rem(i, 2) * 2, 2)] = acc.astype(BF16).reshape(2, 192, width[p])

        remote(part.at[ch, 1, xo], far.at[ch, 1], fs.at[ch, 1], fr.at[ch, 1], right).start()
        remote(part.at[ch, 0, xo], far.at[ch, 0], fs.at[ch, 0], fr.at[ch, 0], left).start()
        remote(part.at[ch, 0, xr], rx.at[ch, 0], rs.at[ch, 0], rr.at[ch, 0], right).start()
        remote(part.at[ch, 1, xl], rx.at[ch, 1], rs.at[ch, 1], rr.at[ch, 1], left).start()

    def relay(p, ch):
        a, wt, part, far, rx, wr, fs, fr, rs, rr = refs[p]
        drain(far.at[ch, 1], fr.at[ch, 1])
        part[ch, 1, xr] = (part[ch, 1, xr].astype(F32) + far[ch, 1].astype(F32)).astype(BF16)
        remote(part.at[ch, 1, xr], rx.at[ch, 2], rs.at[ch, 2], rr.at[ch, 2], right).start()
        drain(far.at[ch, 0], fr.at[ch, 0])
        part[ch, 0, xl] = (part[ch, 0, xl].astype(F32) + far[ch, 0].astype(F32)).astype(BF16)
        remote(part.at[ch, 0, xl], rx.at[ch, 3], rs.at[ch, 3], rr.at[ch, 3], left).start()

    def collect(p, ch):
        a, wt, part, far, rx, wr, fs, fr, rs, rr = refs[p]
        for h, (i, j) in enumerate(((0, 3), (1, 2))):
            drain(rx.at[ch, i], rr.at[ch, i])
            drain(rx.at[ch, j], rr.at[ch, j])
            part[ch, h, x] = (part[ch, h, x].astype(F32) + rx[ch, i].astype(F32) + rx[ch, j].astype(F32)).astype(BF16)
        if p == "q":
            for k in (2, 1, 3):
                yy = lax.rem(y + k, 4)
                cols = pl.ds(pl.multiple_of(lax.rem(yy, 2) * 128, 128), 128)
                remote(part.at[ch, lax.div(yy, 2), x, :, cols], ph_q.at[ch, k - 1],
                       psq.at[ch, k - 1], prq.at[ch, k - 1], dev(dy=k)).start()
        else:
            for k in (2, 1, 3):
                cols = pl.ds(pl.multiple_of(lax.rem(z + k, 4) * 128, 128), 128)
                remote(part.at[ch, :, x, :, cols], ph_o.at[ch, k - 1],
                       pso.at[ch, k - 1], pro.at[ch, k - 1], dev(dz=k)).start()

    def finish(p, ch):
        if p == "q":
            cols = pl.ds(pl.multiple_of(yl * 128, 128), 128)
            total = p_q[ch, yh, x, :, cols].astype(F32)
            for k in range(3):
                drain(ph_q.at[ch, k], prq.at[ch, k])
                total += ph_q[ch, k].astype(F32)
            out_q[:, ch * 128:(ch + 1) * 128] = total.astype(BF16)
        else:
            cols = pl.ds(pl.multiple_of(z * 128, 128), 128)
            for k in range(3):
                drain(ph_o.at[ch, k], pro.at[ch, k])
            give, keep = 1 - yh, yh
            for h in (give, keep):
                total = p_o[ch, h, x, :, cols].astype(F32)
                for k in range(3):
                    total += ph_o[ch, k, h].astype(F32)
                if h is give:
                    swap[0, ch] = total.astype(BF16)
                    remote(swap.at[0, ch], swap.at[1, ch], sws.at[ch], swr.at[ch], dev(dy=2)).start()
                else:
                    out_o[:, pl.ds(pl.multiple_of(yh * 512 + ch * 128, 128), 128)] = total.astype(BF16)

    def settle(ch):
        drain(swap.at[1, ch], swr.at[ch])
        out_o[:, pl.ds(pl.multiple_of((1 - yh) * 512 + ch * 128, 128), 128)] = swap[1, ch]

    n = len(STEPS)
    for i in range(n + 4):
        if i < n:
            compute(*STEPS[i])
        if 1 <= i < n + 1:
            relay(*STEPS[i - 1])
        if 2 <= i < n + 2:
            collect(*STEPS[i - 2])
        if 4 <= i < n + 4:
            finish(*STEPS[i - 4])
    for ch in range(OCH):
        settle(ch)

    q1.wait_send()
    for cp in o1 + [cp for _, cp in q2 + o2] + sibs:
        cp.wait_send()
    for ch in range(QCH):
        drain(snd_q.at[ch, pl.ds(0, 7)], wsq.at[ch])
    for ch in range(OCH):
        drain(snd_o.at[ch, pl.ds(0, 7)], wso.at[ch])
        drain(swap.at[0, ch], sws.at[ch])
    for p, ch in STEPS:
        a, wt, part, far, rx, wr, fs, fr, rs, rr = refs[p]
        for i in range(2):
            drain(far.at[ch, i], fs.at[ch, i])
        for i in range(4):
            drain(rx.at[ch, i], rs.at[ch, i])
        ph, ps = (ph_q, psq) if p == "q" else (ph_o, pso)
        for k in range(3):
            drain(ph.at[ch, k], ps.at[ch, k])


def local(decode_rows, attended, qkv_values, qkv_scales, out_values, out_scales):
    dma = pltpu.SemaphoreType.DMA
    vmem = pltpu.VMEM
    return pl.pallas_call(
        kernel,
        out_shape=(
            jax.ShapeDtypeStruct((192, 1152), BF16),
            jax.ShapeDtypeStruct((192, 1024), BF16),
        ),
        in_specs=[pl.BlockSpec(memory_space=pl.ANY)] * 4 + [pl.BlockSpec(memory_space=pltpu.SMEM)] * 2,
        out_specs=(pl.BlockSpec(memory_space=vmem), pl.BlockSpec(memory_space=vmem)),
        scratch_shapes=[
            vmem((128, 18432), BF16), vmem((128, 16384), BF16),
            vmem((2, 96, 1024), BF16), vmem((4, 96, 512), BF16),
            vmem((4, 2, 2, 96, 1024), BF16), vmem((4, 2, 2, 96, 1024), BF16),
            vmem((QCH, 8, 128, QW), BF16), vmem((OCH, 8, 128, OW), BF16),
            vmem((QCH, 1024, QW), BF16), vmem((OCH, 1024, OW), BF16),
            vmem((QCH, 2, 4, 192, QW), BF16), vmem((OCH, 2, 4, 192, OW), BF16),
            vmem((QCH, 2, 192, QW), BF16), vmem((OCH, 2, 192, OW), BF16),
            vmem((QCH, 4, 192, QW), BF16), vmem((OCH, 4, 192, OW), BF16),
            vmem((QCH, 3, 192, 128), BF16), vmem((OCH, 3, 2, 192, 128), BF16),
            vmem((2, OCH, 192, 128), BF16),
            dma((4,)), dma((4,)), dma((2,)), dma((4,)), dma((8,)), dma((4,)), dma((4,)),
            dma((8,)), dma((4,)), dma((4,)),
            dma((QCH,)), dma((OCH,)), dma((QCH,)), dma((OCH,)),
            dma((QCH, 2)), dma((OCH, 2)), dma((QCH, 2)), dma((OCH, 2)),
            dma((QCH, 4)), dma((OCH, 4)), dma((QCH, 4)), dma((OCH, 4)),
            dma((QCH, 3)), dma((OCH, 3)), dma((QCH, 3)), dma((OCH, 3)),
            dma((OCH,)), dma((OCH,)),
        ],
        compiler_params=pltpu.CompilerParams(
            collective_id=0, has_side_effects=True, vmem_limit_bytes=63 * 2**20
        ),
        cost_estimate=pl.CostEstimate(flops=13_690_000_000, bytes_accessed=20_000_000, transcendentals=0),
        name="project",
    )(
        decode_rows, attended, qkv_values, out_values,
        qkv_scales.astype(F32), out_scales.astype(F32),
    )


def solution(mesh):
    in_specs = (
        P("yz", "gx"),
        P("yz", "gx"),
        P(("gx", "yz"), None),
        P(("gx", "yz"), None),
        P(("gx", "yz"), None),
        P(("gx", "yz"), None),
    )
    out_specs = (P("gx", "yz"), P("gx", "yz"))
    return jax.shard_map(local, mesh=mesh, in_specs=in_specs, out_specs=out_specs, check_vma=False)
```

time: 414 us -> 172 us (0.42)
  waiting for transfers between devices: 239 us -> 0 us
  Pallas kernels: 0 us -> 165 us
  local copies, waits for them, and re-layouts: 77 us -> 3.58 us
  other arithmetic: 34.1 us -> 2.41 us
  matrix products: 25.1 us -> 0 us
  starting transfers between devices: 23.7 us -> 0 us
  between operations: 13.8 us -> 0.64 us
    pallas_call x0 -> x1, Pallas kernels: none -> 165 us  [local(): pl.pallas_call(kernel, out_shape=(jax.ShapeDtypeStruct((192, 1152), BF16)...]
    all_to_all x4 -> x0, waiting for transfers between devices: 137 us -> none  [the longest x1 75.3 us: local(): lax.all_to_all(out_values, 'yz', split_axis=1, concat_axis=0, tiled=True)]
    unnamed x6 -> x0, waiting for transfers between devices: 102 us -> none
    unnamed x12 -> x2, local copies, waits for them, and re-layouts: 41.7 us -> 3.58 us
    convert_element_type x6 -> x2, other arithmetic: 32.8 us -> 2.41 us  [the longest x1 1.24 us: local(): qkv_scales.astype(F32)]
    dot_general x2 -> x0, matrix products: 25.1 us -> none  [the longest x1 13 us: local(): jnp.dot(all_hidden, qkv_weight, preferred_element_type=jnp.float32)]
    all_to_all x4 -> x0, starting transfers between devices: 23.3 us -> none  [the longest x1 7.84 us: local(): lax.all_to_all(out_scales, 'yz', split_axis=1, concat_axis=0, tiled=True)]
    convert_element_type x4 -> x0, local copies, waits for them, and re-layouts: 19.5 us -> none  [the longest x2 19.4 us: dequantize(): values.reshape(rows // TILE, TILE, cols // TILE, TILE).astype(jnp.float32)]
  transfers between devices with their start and end apart: 8 -> 0, of which waited for: 3 -> 0; matrix products, arithmetic and copies ran while one was open for 32% -> 0% of each run, Pallas kernels for 0% -> 0%
where the time goes in v1:
time: 172 us
  Pallas kernels  165 us (96%)
  local copies, waits for them, and re-layouts  3.58 us (2%)
  other arithmetic  2.41 us (1%)
    pallas_call x1, Pallas kernels, local(): pl.pallas_call(kernel, out_shape=(jax.ShapeDtypeStruct((192, 1152), BF16)...  165 us
    unnamed x2, local copies, waits for them, and re-layouts  3.58 us

profile of v1, /device:TPU:1, one launch (start us, length us, event | category | flops | bytes accessed | tf_op | source)
XLA Modules:
  0.0 171.7 jit_solution(14347306064240932899)
XLA Ops:
  0.6 1.2 convert_element_type.7.sc_o
  1.8 1.2 convert_element_type.6.sc_q
  3.0 165.1 %project.1 = (bf16[192,1152]{1,0:T(8,128)(2,1)}, bf16[192,1024]{1,0:T(8,128)(2,1)}) custom-call(bf16[96,2048]{1,0:T(8,128)(2,1)} %rows_q.1, bf16[96,2048]{1,0:T(8,128)(2,1)} %rows_o.1, bf16[128,18432]{1,0:T(8,128)(2,1)} %val_q.1, bf16[128,16384]{1,0:T(8,128)(2,1)} %val_o.1, f32[1,144]{1,0:T(1,128)} %convert_element_type.6.sc_q, ...), custom_call_target="tpu_custom_call" | custom-call | flops 13690000384 | bytes 20000000 | tf_op jit(solution)/shard_map/project/pallas_call | solution.py:275
  168.1 1.8 %copy.10 = bf16[192,1152]{1,0:T(8,128)(2,1)} copy(bf16[192,1152]{1,0:T(8,128)(2,1)} %get-tuple-element.4) | data formatting | bytes 884736
  169.9 1.8 %copy.11 = bf16[192,1024]{1,0:T(8,128)(2,1)} copy(bf16[192,1024]{1,0:T(8,128)(2,1)} %get-tuple-element.5) | data formatting | bytes 786432

commit v2 on v1

v2 whole, which is shorter than its diff:
```python
import jax
import jax.numpy as jnp
from jax import lax
from jax.experimental import pallas as pl
from jax.experimental.pallas import tpu as pltpu
from jax.sharding import PartitionSpec as P

MESH = pl.DeviceIdType.MESH
F32 = jnp.float32
BF16 = jnp.bfloat16

QCH, QW = 9, 256
OCH, OW = 4, 512
SWAPPED = (("o", 3), ("q", 4), ("q", 5), ("q", 6), ("q", 7), ("q", 8),)
CHUNKS = tuple(("q", i) for i in range(QCH)) + tuple(("o", i) for i in range(OCH))
PLACE = {}
for _p in "qo":
    for _kind in (False, True):
        for _i, _t in enumerate(t for t in CHUNKS if t[0] == _p and (t in SWAPPED) == _kind):
            PLACE[_t] = _i
NQS, NOS = (sum(t[0] == p for t in SWAPPED) for p in "qo")
OPS = (
    ("q1",), ("o1",), ("w", "q", 0), ("q2",), ("o2",), ("w", "o", 0), ("w", "q", 1), ("w", "q", 2),
    ("w", "o", 1), ("w", "q", 3), ("w", "q", 4), ("w", "o", 2), ("w", "q", 5), ("w", "q", 6), ("w", "o", 3),
    ("w", "q", 7), ("w", "q", 8), ("F", "q", 2), ("F", "o", 1), ("F", "o", 2), ("F", "o", 3), ("F", "q", 1),
    ("F", "q", 3), ("c", "q", 0), ("c", "q", 1), ("c", "o", 0), ("r", "q", 0), ("c", "q", 2), ("r", "q", 1),
    ("c", "q", 3), ("r", "o", 0), ("c", "o", 1), ("c", "q", 4), ("k", "q", 0), ("r", "q", 2), ("c", "o", 2),
    ("k", "q", 1), ("c", "q", 5), ("r", "q", 3), ("c", "q", 6), ("k", "o", 0), ("c", "o", 3), ("r", "q", 4),
    ("c", "q", 7), ("r", "o", 1), ("f", "q", 0), ("c", "q", 8), ("f", "q", 1), ("k", "q", 2), ("r", "q", 5),
    ("f", "o", 0), ("r", "o", 2), ("r", "q", 6), ("r", "o", 3), ("k", "q", 4), ("k", "q", 3), ("r", "q", 7),
    ("k", "o", 3), ("r", "q", 8), ("k", "o", 1), ("k", "o", 2), ("f", "q", 2), ("f", "q", 4), ("k", "q", 5),
    ("f", "o", 1), ("k", "q", 6), ("f", "o", 3), ("f", "q", 3), ("f", "q", 5), ("f", "o", 2), ("k", "q", 7),
    ("f", "q", 6), ("k", "q", 8), ("f", "q", 7), ("f", "q", 8),
)


def kernel(
    rows_q, rows_o, val_q, val_o, scale_q, scale_o,
    out_q, out_o,
    in_q, in_o, x_q, x_o, a_q, a_o, snd_q, snd_o, w_q, w_o, p_q, p_o,
    far_q, far_o, far_qs, far_os, rx_q, rx_o, rx_qs, rx_os, ph_q, ph_o, swap, scf_q, scf_o, sc_q, sc_o,
    ld, s1s, s1q, s1o, s2s, s2q, s2o, sbs, sbq, sbo,
    wsq, wso, wrq, wro, fsq, fso, frq, fro, rsq, rso, rrq, rro, psq, pso, prq, pro, sws, swr,
):
    g = lax.axis_index("gx")
    w = lax.axis_index("yz")
    x, yh = lax.rem(g, 4), lax.div(g, 4)
    c, yl, z = lax.rem(w, 2), lax.rem(lax.div(w, 2), 2), lax.div(w, 4)
    y = yh * 2 + yl

    def dev(dx=0, dy=0, dz=0, dc=0):
        xx, yy, zz, cc = (lax.rem(x + dx, 4), lax.rem(y + dy, 4), lax.rem(z + dz, 4), lax.rem(c + dc, 2))
        return (lax.div(yy, 2) * 4 + xx, zz * 4 + lax.rem(yy, 2) * 2 + cc)

    mate = (g, z * 4 + (1 - yl) * 2 + c)
    sib = dev(dc=1)

    def remote(src, dst, ssem, rsem, to):
        return pltpu.make_async_remote_copy(
            src_ref=src, dst_ref=dst, send_sem=ssem, recv_sem=rsem, device_id=to, device_id_type=MESH
        )

    def drain(ref, sem):
        pltpu.make_async_copy(ref, ref, sem).wait()

    loads = []
    for half in range(2):
        for zz in range(4):
            loads.append(pltpu.make_async_copy(
                rows_q.at[:, pl.ds(zz * 512 + half * 256, 256)],
                x_q.at[half, :, pl.ds(zz * 256, 256)], ld.at[0]))
    for zz in range(4):
        loads.append(pltpu.make_async_copy(
            rows_o.at[:, pl.ds(zz * 512, 512)], x_o.at[zz], ld.at[1]))
    loads.append(pltpu.make_async_copy(val_q, in_q, ld.at[2]))
    loads.append(pltpu.make_async_copy(val_o, in_o, ld.at[3]))
    for cp in loads:
        cp.start()

    scf_q[...] = scale_q[...].astype(F32)
    scf_o[...] = scale_o[...].astype(F32)
    for src, dst, sem in ((scf_q, sc_q, ld.at[4]), (scf_o, sc_o, ld.at[5])):
        cp = pltpu.make_async_copy(src, dst, sem)
        cp.start()
        loads.append(cp)

    peers = [dev(dy=dy, dz=dz) for dy in range(4) for dz in range(4) if (dy, dz) != (0, 0)]
    peers += [dev(dz=dz, dc=1) for dz in range(4)]
    peers += [dev(dy=dy, dc=1) for dy in range(1, 4)]
    peers += [dev(dx=1), dev(dx=2), dev(dx=3)]
    barrier = pltpu.get_barrier_semaphore()
    for peer in peers:
        pl.semaphore_signal(barrier, inc=1, device_id=peer, device_id_type=MESH)
    pl.semaphore_wait(barrier, len(peers))

    own_cols = pl.ds(pl.multiple_of(yh * 512, 512), 512)
    pending = []
    stage = {}

    def first_q():
        drain(x_q, ld.at[0])
        cp = remote(x_q.at[1 - yl], a_q.at[z, yl, c], s1s.at[0], s1q.at[0], mate)
        cp.start()
        here = pltpu.make_async_copy(x_q.at[yl], a_q.at[z, yl, c], s1q.at[1])
        here.start()
        stage["q"] = [cp], here

    def first_o():
        drain(x_o, ld.at[1])
        cps = []
        for k in (2, 1, 3):
            cp = remote(x_o.at[lax.rem(z + k, 4)], a_o.at[z, yl, c, :, own_cols], s1s.at[k], s1o.at[k], dev(dz=k))
            cp.start()
            cps.append(cp)
        here = pltpu.make_async_copy(x_o.at[z], a_o.at[z, yl, c, :, own_cols], s1o.at[0])
        here.start()
        stage["o"] = cps, here

    def second(p):
        cps, here = stage[p]
        for cp in cps:
            cp.wait_recv()
        here.wait()
        pending.extend(cps)
        if p == "q":
            mine, ss, rs, bs, br = a_q.at[z, :, c], 0, s2q, 0, sbq
        else:
            mine, ss, rs, bs, br = a_o.at[:, yl, c, :, own_cols], 4, s2o, 4, sbo
        for k in (2, 1, 3):
            cp = remote(mine, mine, s2s.at[ss + k], rs.at[k], dev(dz=k) if p == "q" else dev(dy=k))
            cp.start()
            stage[p, k] = cp
            pending.append(cp)
        cp = remote(mine, mine, sbs.at[bs], br.at[0], sib)
        cp.start()
        stage[p, "sib"] = [cp]

    def forward(p, k):
        stage[p, k].wait_recv()
        if p == "q":
            part = a_q.at[lax.rem(z + 4 - k, 4), :, c]
            cp = remote(part, part, sbs.at[k], sbq.at[k], sib)
        else:
            yy = lax.rem(y + 4 - k, 4)
            part = a_o.at[:, lax.rem(yy, 2), c, :, pl.ds(pl.multiple_of(lax.div(yy, 2) * 512, 512), 512)]
            cp = remote(part, part, sbs.at[4 + k], sbo.at[k], sib)
        cp.start()
        stage[p, "sib"].append(cp)

    def rows_ready(p):
        for cp in stage.pop((p, "sib"), []):
            cp.wait_recv()
            pending.append(cp)

    def weights_q(ch):
        @pl.loop(0, 8)
        def _(d):
            for half in range(2):
                block = lax.div(d, 2) * 4 + half * 2 + lax.rem(d, 2)
                col = pl.multiple_of(block * 1152 + ch * 128, 128)
                s = sc_q[0, block * 9 + ch]
                snd_q[ch, d, :, half * 128:(half + 1) * 128] = (
                    in_q[:, pl.ds(col, 128)].astype(F32) * s).astype(BF16)
        here = pl.ds(pl.multiple_of((z * 2 + c) * 128, 128), 128)
        for k, dc in ((2, 0), (2, 1), (1, 0), (3, 0), (1, 1), (3, 1), (0, 1)):
            slot = lax.rem(z + k, 4) * 2 + lax.rem(c + dc, 2)
            remote(snd_q.at[ch, slot], w_q.at[ch, here], wsq.at[ch], wrq.at[ch], dev(dz=k, dc=dc)).start()
        pltpu.make_async_copy(snd_q.at[ch, z * 2 + c], w_q.at[ch, here], wrq.at[ch]).start()

    def weights_o(ch):
        @pl.loop(0, 8)
        def _(d):
            for zz in range(4):
                block = zz * 4 + lax.rem(d, 4)
                tile = block * 8 + lax.div(d, 4) * 4 + ch
                col = pl.multiple_of(tile * 128, 128)
                s = sc_o[0, tile]
                snd_o[ch, d, :, zz * 128:(zz + 1) * 128] = (
                    in_o[:, pl.ds(col, 128)].astype(F32) * s).astype(BF16)
        here = pl.ds(pl.multiple_of((y * 2 + c) * 128, 128), 128)
        for k, dc in ((2, 0), (2, 1), (1, 0), (3, 0), (1, 1), (3, 1), (0, 1)):
            slot = lax.rem(y + k, 4) * 2 + lax.rem(c + dc, 2)
            remote(snd_o.at[ch, slot], w_o.at[ch, here], wso.at[ch], wro.at[ch], dev(dy=k, dc=dc)).start()
        pltpu.make_async_copy(snd_o.at[ch, y * 2 + c], w_o.at[ch, here], wro.at[ch]).start()

    loaded = set()

    def weights(p, ch):
        if p not in loaded:
            loaded.add(p)
            i = "qo".index(p)
            drain((in_q, in_o)[i], ld.at[2 + i])
            loads[-2 + i].wait()
        (weights_q if p == "q" else weights_o)(ch)

    class Chunk:
        def __init__(self, p, ch):
            swapped = (p, ch) in SWAPPED
            at = PLACE[p, ch]
            self.p, self.ch, self.swapped = p, ch, swapped
            self.part = p_q if p == "q" else p_o
            if p == "q":
                self.far, self.rx = (far_qs, rx_qs) if swapped else (far_q, rx_q)
                self.far_sems, self.rx_sems = (fsq, frq), (rsq, rrq)
            else:
                self.far, self.rx = (far_os, rx_os) if swapped else (far_o, rx_o)
                self.far_sems, self.rx_sems = (fso, fro), (rso, rro)
            self.far, self.rx = self.far.at[at], self.rx.at[at]
            if not swapped:
                self.me, self.right, self.left = x, dev(dx=1), dev(dx=3)
            elif p == "q":
                self.me, self.right, self.left = y, dev(dy=1), dev(dy=3)
            else:
                self.me, self.right, self.left = z, dev(dz=1), dev(dz=3)

        def block(self, ahead, half):
            to = lax.rem(self.me + ahead, 4)
            if not self.swapped:
                return self.part.at[self.ch, half, to]
            if self.p == "q":
                cols = pl.ds(pl.multiple_of(lax.rem(to, 2) * 128, 128), 128)
                return self.part.at[self.ch, lax.div(to, 2), pl.ds(2 * half, 2), :, cols]
            cols = pl.ds(pl.multiple_of(to * 128, 128), 128)
            return self.part.at[self.ch, half, :, :, cols]

        def send_far(self, src, half, to):
            ss, rs = self.far_sems
            remote(src, self.far.at[half], ss.at[self.ch, half], rs.at[self.ch, half], to).start()

        def send_sum(self, src, slot, to):
            ss, rs = self.rx_sems
            remote(src, self.rx.at[slot], ss.at[self.ch, slot], rs.at[self.ch, slot], to).start()

    def compute(p, ch):
        t = Chunk(p, ch)
        a, wt, wr, wide = (a_q, w_q, wrq, QW) if p == "q" else (a_o, w_o, wro, OW)
        rows_ready(p)
        drain(wt.at[ch], wr.at[ch])

        @pl.loop(0, 4)
        def _(i):
            lhs = a[i].reshape(384, 1024)
            acc = jnp.dot(lhs, wt[ch], preferred_element_type=F32)
            t.part[ch, lax.div(i, 2), pl.ds(lax.rem(i, 2) * 2, 2)] = acc.astype(BF16).reshape(2, 192, wide)

        t.send_far(t.block(2, 1), 1, t.right)
        t.send_far(t.block(2, 0), 0, t.left)
        t.send_sum(t.block(1, 0), 0, t.right)
        t.send_sum(t.block(3, 1), 1, t.left)

    def relay(p, ch):
        t = Chunk(p, ch)
        for half, ahead, slot, to in ((1, 1, 2, t.right), (0, 3, 3, t.left)):
            drain(t.far.at[half], t.far_sems[1].at[ch, half])
            own = t.block(ahead, half)
            own[...] = (own[...].astype(F32) + t.far[half].astype(F32)).astype(BF16)
            t.send_sum(own, slot, to)

    def collect(p, ch):
        t = Chunk(p, ch)
        for half, (i, j) in enumerate(((0, 3), (1, 2))):
            drain(t.rx.at[i], t.rx_sems[1].at[ch, i])
            drain(t.rx.at[j], t.rx_sems[1].at[ch, j])
            own = t.block(0, half)
            own[...] = (own[...].astype(F32) + t.rx[i].astype(F32) + t.rx[j].astype(F32)).astype(BF16)
        for k in (2, 1, 3):
            xx, yy, zz = lax.rem(x + k, 4), lax.rem(y + k, 4), lax.rem(z + k, 4)
            if p == "q":
                hh, ll = (yh, yl) if t.swapped else (lax.div(yy, 2), lax.rem(yy, 2))
                src = p_q.at[ch, hh, xx if t.swapped else x, :, pl.ds(pl.multiple_of(ll * 128, 128), 128)]
                to = dev(dx=k) if t.swapped else dev(dy=k)
                remote(src, ph_q.at[ch, k - 1], psq.at[ch, k - 1], prq.at[ch, k - 1], to).start()
            else:
                cols = pl.ds(pl.multiple_of((z if t.swapped else zz) * 128, 128), 128)
                src = p_o.at[ch, :, xx if t.swapped else x, :, cols]
                to = dev(dx=k) if t.swapped else dev(dz=k)
                remote(src, ph_o.at[ch, k - 1], pso.at[ch, k - 1], pro.at[ch, k - 1], to).start()

    def finish(p, ch):
        if p == "q":
            cols = pl.ds(pl.multiple_of(yl * 128, 128), 128)
            total = p_q[ch, yh, x, :, cols].astype(F32)
            for k in range(3):
                drain(ph_q.at[ch, k], prq.at[ch, k])
                total += ph_q[ch, k].astype(F32)
            out_q[:, ch * 128:(ch + 1) * 128] = total.astype(BF16)
        else:
            cols = pl.ds(pl.multiple_of(z * 128, 128), 128)
            for k in range(3):
                drain(ph_o.at[ch, k], pro.at[ch, k])
            give, keep = 1 - yh, yh
            for h in (give, keep):
                total = p_o[ch, h, x, :, cols].astype(F32)
                for k in range(3):
                    total += ph_o[ch, k, h].astype(F32)
                if h is give:
                    swap[0, ch] = total.astype(BF16)
                    remote(swap.at[0, ch], swap.at[1, ch], sws.at[ch], swr.at[ch], dev(dy=2)).start()
                else:
                    out_o[:, pl.ds(pl.multiple_of(yh * 512 + ch * 128, 128), 128)] = total.astype(BF16)

    def settle(ch):
        drain(swap.at[1, ch], swr.at[ch])
        out_o[:, pl.ds(pl.multiple_of((1 - yh) * 512 + ch * 128, 128), 128)] = swap[1, ch]

    todo = {
        "q1": first_q, "o1": first_o, "q2": lambda: second("q"), "o2": lambda: second("o"),
        "F": forward, "w": weights, "c": compute, "r": relay, "k": collect, "f": finish,
    }
    for op in OPS:
        todo[op[0]](*op[1:])
    for ch in range(OCH):
        settle(ch)

    for cp in pending:
        cp.wait_send()
    for ch in range(QCH):
        drain(snd_q.at[ch, pl.ds(0, 7)], wsq.at[ch])
    for ch in range(OCH):
        drain(snd_o.at[ch, pl.ds(0, 7)], wso.at[ch])
        drain(swap.at[0, ch], sws.at[ch])
    for p, ch in CHUNKS:
        t = Chunk(p, ch)
        for i in range(2):
            drain(t.far.at[i], t.far_sems[0].at[ch, i])
        for i in range(4):
            drain(t.rx.at[i], t.rx_sems[0].at[ch, i])
        ph, ps = (ph_q, psq) if p == "q" else (ph_o, pso)
        for k in range(3):
            drain(ph.at[ch, k], ps.at[ch, k])


def place_kernel(a, b, out_a, out_b):
    out_a[...] = a[...]
    out_b[...] = b[...]


def local(decode_rows, attended, qkv_values, qkv_scales, out_values, out_scales):
    dma = pltpu.SemaphoreType.DMA
    vmem = pltpu.VMEM
    sums = pl.pallas_call(
        kernel,
        out_shape=(
            jax.ShapeDtypeStruct((192, 1152), BF16),
            jax.ShapeDtypeStruct((192, 1024), BF16),
        ),
        in_specs=[pl.BlockSpec(memory_space=pl.ANY)] * 4 + [pl.BlockSpec(memory_space=vmem)] * 2,
        out_specs=(pl.BlockSpec(memory_space=vmem), pl.BlockSpec(memory_space=vmem)),
        scratch_shapes=[
            vmem((128, 18432), BF16), vmem((128, 16384), BF16),
            vmem((2, 96, 1024), BF16), vmem((4, 96, 512), BF16),
            vmem((4, 2, 2, 96, 1024), BF16), vmem((4, 2, 2, 96, 1024), BF16),
            vmem((QCH, 8, 128, QW), BF16), vmem((OCH, 8, 128, OW), BF16),
            vmem((QCH, 1024, QW), BF16), vmem((OCH, 1024, OW), BF16),
            vmem((QCH, 2, 4, 192, QW), BF16), vmem((OCH, 2, 4, 192, OW), BF16),
            vmem((QCH - NQS, 2, 192, QW), BF16), vmem((OCH - NOS, 2, 192, OW), BF16),
            vmem((NQS, 2, 2, 192, 128), BF16), vmem((NOS, 2, 4, 192, 128), BF16),
            vmem((QCH - NQS, 4, 192, QW), BF16), vmem((OCH - NOS, 4, 192, OW), BF16),
            vmem((NQS, 4, 2, 192, 128), BF16), vmem((NOS, 4, 4, 192, 128), BF16),
            vmem((QCH, 3, 192, 128), BF16), vmem((OCH, 3, 2, 192, 128), BF16),
            vmem((2, OCH, 192, 128), BF16),
            vmem((1, 144), F32), vmem((1, 128), F32), pltpu.SMEM((1, 144), F32), pltpu.SMEM((1, 128), F32),
            dma((6,)), dma((4,)), dma((2,)), dma((4,)), dma((8,)), dma((4,)), dma((4,)),
            dma((8,)), dma((4,)), dma((4,)),
            dma((QCH,)), dma((OCH,)), dma((QCH,)), dma((OCH,)),
            dma((QCH, 2)), dma((OCH, 2)), dma((QCH, 2)), dma((OCH, 2)),
            dma((QCH, 4)), dma((OCH, 4)), dma((QCH, 4)), dma((OCH, 4)),
            dma((QCH, 3)), dma((OCH, 3)), dma((QCH, 3)), dma((OCH, 3)),
            dma((OCH,)), dma((OCH,)),
        ],
        compiler_params=pltpu.CompilerParams(
            collective_id=0, has_side_effects=True, vmem_limit_bytes=63 * 2**20
        ),
        cost_estimate=pl.CostEstimate(flops=13_690_000_000, bytes_accessed=20_000_000, transcendentals=0),
        name="project",
    )(
        decode_rows, attended, qkv_values, out_values,
        qkv_scales, out_scales,
    )
    return pl.pallas_call(
        place_kernel,
        out_shape=tuple(jax.ShapeDtypeStruct(s.shape, BF16) for s in sums),
        in_specs=[pl.BlockSpec(memory_space=vmem)] * 2,
        out_specs=tuple([pl.BlockSpec(memory_space=vmem)] * 2),
        compiler_params=pltpu.CompilerParams(vmem_limit_bytes=4 * 2**20),
        name="place",
    )(*sums)


def solution(mesh):
    in_specs = (
        P("yz", "gx"),
        P("yz", "gx"),
        P(("gx", "yz"), None),
        P(("gx", "yz"), None),
        P(("gx", "yz"), None),
        P(("gx", "yz"), None),
    )
    out_specs = (P("gx", "yz"), P("gx", "yz"))
    return jax.shard_map(local, mesh=mesh, in_specs=in_specs, out_specs=out_specs, check_vma=False)
```

time: 172 us -> 135 us (0.78)
  Pallas kernels: 165 us -> 132 us
  other arithmetic: 2.41 us -> 0 us
    pallas_call x1, Pallas kernels: 165 us -> 131 us  [local(): pl.pallas_call(kernel, out_shape=(jax.ShapeDtypeStruct((192, 1152), BF16)...]
    convert_element_type x2 -> x0, other arithmetic: 2.41 us -> none  [the longest x1 1.24 us: local(): qkv_scales.astype(F32)]
    unnamed x2 -> x4, local copies, waits for them, and re-layouts: 3.58 us -> 2 us
where the time goes in v2:
time: 135 us
  Pallas kernels  132 us (98%)
  local copies, waits for them, and re-layouts  2 us (1%)
    pallas_call x1, Pallas kernels, local(): pl.pallas_call(kernel, out_shape=(jax.ShapeDtypeStruct((192, 1152), BF16)...  131 us

profile of v2, /device:TPU:1, one launch (start us, length us, event | category | flops | bytes accessed | tf_op | source)
XLA Modules:
  0.0 134.6 jit_solution(15976150529833951751)
XLA Ops:
  0.6 131.0 %project.1 = (bf16[192,1152]{1,0:T(8,128)(2,1)}, bf16[192,1024]{1,0:T(8,128)(2,1)}) custom-call(bf16[96,2048]{1,0:T(8,128)(2,1)} %rows_q.1, bf16[96,2048]{1,0:T(8,128)(2,1)} %rows_o.1, bf16[128,18432]{1,0:T(8,128)(2,1)} %val_q.1, bf16[128,16384]{1,0:T(8,128)(2,1)} %val_o.1, bf16[1,144]{1,0:T(2,128)(2,1)} %scale_q.1, bf16[1,128]{1,0:T(2,128)(2,1)} %scale_o.1), custom_call_target="tpu_custom_call" | custom-call | flops 13690000384 | bytes 20000000 | tf_op jit(solution)/shard_map/project/pallas_call | solution.py:341
  131.7 0.0 copy-start
  131.7 1.0 copy-done
  132.7 0.0 copy-start.1
  132.7 1.0 copy-done.1
  133.7 0.9 place.1
Async XLA Ops:
  131.7 1.0 copy-start
  132.7 1.0 copy-start.1

commit v3 on v2

--- a/solution.py
+++ b/solution.py
@@ -11,7 +11,7 @@
 
 QCH, QW = 9, 256
 OCH, OW = 4, 512
-SWAPPED = (("o", 3), ("q", 4), ("q", 5), ("q", 6), ("q", 7), ("q", 8),)
+SWAPPED = (("o", 1), ("q", 0), ("q", 1), ("q", 2), ("q", 4), ("q", 6),)
 CHUNKS = tuple(("q", i) for i in range(QCH)) + tuple(("o", i) for i in range(OCH))
 PLACE = {}
 for _p in "qo":
@@ -20,17 +20,18 @@
             PLACE[_t] = _i
 NQS, NOS = (sum(t[0] == p for t in SWAPPED) for p in "qo")
 OPS = (
-    ("q1",), ("o1",), ("w", "q", 0), ("q2",), ("o2",), ("w", "o", 0), ("w", "q", 1), ("w", "q", 2),
-    ("w", "o", 1), ("w", "q", 3), ("w", "q", 4), ("w", "o", 2), ("w", "q", 5), ("w", "q", 6), ("w", "o", 3),
-    ("w", "q", 7), ("w", "q", 8), ("F", "q", 2), ("F", "o", 1), ("F", "o", 2), ("F", "o", 3), ("F", "q", 1),
-    ("F", "q", 3), ("c", "q", 0), ("c", "q", 1), ("c", "o", 0), ("r", "q", 0), ("c", "q", 2), ("r", "q", 1),
-    ("c", "q", 3), ("r", "o", 0), ("c", "o", 1), ("c", "q", 4), ("k", "q", 0), ("r", "q", 2), ("c", "o", 2),
-    ("k", "q", 1), ("c", "q", 5), ("r", "q", 3), ("c", "q", 6), ("k", "o", 0), ("c", "o", 3), ("r", "q", 4),
-    ("c", "q", 7), ("r", "o", 1), ("f", "q", 0), ("c", "q", 8), ("f", "q", 1), ("k", "q", 2), ("r", "q", 5),
-    ("f", "o", 0), ("r", "o", 2), ("r", "q", 6), ("r", "o", 3), ("k", "q", 4), ("k", "q", 3), ("r", "q", 7),
-    ("k", "o", 3), ("r", "q", 8), ("k", "o", 1), ("k", "o", 2), ("f", "q", 2), ("f", "q", 4), ("k", "q", 5),
-    ("f", "o", 1), ("k", "q", 6), ("f", "o", 3), ("f", "q", 3), ("f", "q", 5), ("f", "o", 2), ("k", "q", 7),
-    ("f", "q", 6), ("k", "q", 8), ("f", "q", 7), ("f", "q", 8),
+    ("o1",), ("q1",), ("w", "o", 0), ("o2",), ("q2",), ("F", "q", 0, 1), ("F", "q", 0, 3), ("w", "q", 3),
+    ("w", "o", 3), ("F", "q", 1, 1), ("F", "q", 1, 3), ("w", "q", 7), ("w", "q", 8), ("F", "q", 0, 2),
+    ("w", "q", 5), ("w", "q", 4), ("w", "q", 1), ("F", "q", 1, 2), ("F", "o", 0, 1), ("F", "o", 0, 3),
+    ("c", "q", 3), ("c", "q", 7), ("w", "o", 2), ("w", "o", 1), ("r", "q", 3), ("c", "q", 8), ("r", "q", 7),
+    ("F", "o", 0, 2), ("k", "q", 3), ("w", "q", 0), ("c", "q", 5), ("r", "q", 8), ("c", "o", 0),
+    ("c", "o", 3), ("k", "q", 7), ("r", "q", 5), ("c", "q", 4), ("w", "q", 2), ("w", "q", 6), ("k", "q", 8),
+    ("c", "q", 1), ("c", "o", 2), ("r", "o", 0), ("c", "q", 0), ("c", "o", 1), ("f", "q", 3), ("c", "q", 2),
+    ("r", "o", 3), ("f", "q", 7), ("r", "q", 4), ("c", "q", 6), ("k", "q", 5), ("f", "q", 8), ("r", "q", 1),
+    ("r", "o", 1), ("r", "o", 2), ("r", "q", 0), ("r", "q", 2), ("k", "o", 1), ("k", "o", 0), ("k", "q", 4),
+    ("k", "o", 3), ("r", "q", 6), ("k", "o", 2), ("f", "o", 0), ("f", "q", 5), ("k", "q", 1), ("f", "o", 1),
+    ("f", "o", 3), ("k", "q", 0), ("f", "q", 4), ("k", "q", 2), ("f", "q", 1), ("f", "o", 2), ("k", "q", 6),
+    ("f", "q", 0), ("f", "q", 2), ("f", "q", 6),
 )
 
 
@@ -39,7 +40,7 @@
     out_q, out_o,
     in_q, in_o, x_q, x_o, a_q, a_o, snd_q, snd_o, w_q, w_o, p_q, p_o,
     far_q, far_o, far_qs, far_os, rx_q, rx_o, rx_qs, rx_os, ph_q, ph_o, swap, scf_q, scf_o, sc_q, sc_o,
-    ld, s1s, s1q, s1o, s2s, s2q, s2o, sbs, sbq, sbo,
+    ld, s1s, s1q, s1o, s2s, s2r,
     wsq, wso, wrq, wro, fsq, fso, frq, fro, rsq, rso, rrq, rro, psq, pso, prq, pro, sws, swr,
 ):
     g = lax.axis_index("gx")
@@ -104,6 +105,7 @@
         here = pltpu.make_async_copy(x_q.at[yl], a_q.at[z, yl, c], s1q.at[1])
         here.start()
         stage["q"] = [cp], here
+        stream("q", 0, x_q.at[yl])
 
     def first_o():
         drain(x_o, ld.at[1])
@@ -116,41 +118,61 @@
         here.start()
         stage["o"] = cps, here
 
+    def piece(p, sid, back):
+        if p == "q":
+            return a_q.at[lax.rem(z + 4 - back, 4), yl if sid == 0 else 1 - yl, c]
+        yy = lax.rem(y + 4 - back, 4)
+        return a_o.at[:, lax.rem(yy, 2), c, :, pl.ds(pl.multiple_of(lax.div(yy, 2) * 512, 512), 512)]
+
+    def half(p, ref, i):
+        return ref.at[pl.ds(48 * i, 48)] if p == "q" else ref.at[pl.ds(2 * i, 2)]
+
+    def along(p, k):
+        return dev(dz=k) if p == "q" else dev(dy=k)
+
+    def push(p, sid, src, dst, slot, to):
+        row = sid if p == "q" else 2
+        cp = remote(src, dst, s2s.at[row, slot], s2r.at[row, slot], to)
+        cp.start()
+        pending.append(cp)
+
+    def arrived(p, sid, ref, slot):
+        drain(ref, s2r.at[sid if p == "q" else 2, slot])
+
+    def stream(p, sid, src):
+        mine = piece(p, sid, 0)
+        push(p, sid, src, mine, 0, along(p, 1))
+        push(p, sid, src, mine, 1, along(p, 3))
+        push(p, sid, src, mine, 4, sib)
+
     def second(p):
         cps, here = stage[p]
         for cp in cps:
             cp.wait_recv()
         here.wait()
         pending.extend(cps)
-        if p == "q":
-            mine, ss, rs, bs, br = a_q.at[z, :, c], 0, s2q, 0, sbq
+        sid = 1 if p == "q" else 0
+        stream(p, sid, piece(p, sid, 0))
+
+    def forward(p, sid, k):
+        part = piece(p, sid, k)
+        if k == 2:
+            arrived(p, sid, half(p, part, 0), 2)
+            arrived(p, sid, half(p, part, 1), 3)
         else:
-            mine, ss, rs, bs, br = a_o.at[:, yl, c, :, own_cols], 4, s2o, 4, sbo
-        for k in (2, 1, 3):
-            cp = remote(mine, mine, s2s.at[ss + k], rs.at[k], dev(dz=k) if p == "q" else dev(dy=k))
-            cp.start()
-            stage[p, k] = cp
-            pending.append(cp)
-        cp = remote(mine, mine, sbs.at[bs], br.at[0], sib)
-        cp.start()
-        stage[p, "sib"] = [cp]
-
-    def forward(p, k):
-        stage[p, k].wait_recv()
-        if p == "q":
-            part = a_q.at[lax.rem(z + 4 - k, 4), :, c]
-            cp = remote(part, part, sbs.at[k], sbq.at[k], sib)
-        else:
-            yy = lax.rem(y + 4 - k, 4)
-            part = a_o.at[:, lax.rem(yy, 2), c, :, pl.ds(pl.multiple_of(lax.div(yy, 2) * 512, 512), 512)]
-            cp = remote(part, part, sbs.at[4 + k], sbo.at[k], sib)
-        cp.start()
-        stage[p, "sib"].append(cp)
+            i = k // 2
+            arrived(p, sid, part, i)
+            push(p, sid, half(p, part, i), half(p, part, i), 2 + i, along(p, k))
+        push(p, sid, part, part, 4 + k, sib)
+
+    ready = set()
 
     def rows_ready(p):
-        for cp in stage.pop((p, "sib"), []):
-            cp.wait_recv()
-            pending.append(cp)
+        if p not in ready:
+            ready.add(p)
+            for sid in range(2 if p == "q" else 1):
+                for k in range(4):
+                    arrived(p, sid, piece(p, sid, 0), 4 + k)
 
     def weights_q(ch):
         @pl.loop(0, 8)
@@ -360,8 +382,7 @@
             vmem((QCH, 3, 192, 128), BF16), vmem((OCH, 3, 2, 192, 128), BF16),
             vmem((2, OCH, 192, 128), BF16),
             vmem((1, 144), F32), vmem((1, 128), F32), pltpu.SMEM((1, 144), F32), pltpu.SMEM((1, 128), F32),
-            dma((6,)), dma((4,)), dma((2,)), dma((4,)), dma((8,)), dma((4,)), dma((4,)),
-            dma((8,)), dma((4,)), dma((4,)),
+            dma((6,)), dma((4,)), dma((2,)), dma((4,)), dma((3, 8)), dma((3, 8)),
             dma((QCH,)), dma((OCH,)), dma((QCH,)), dma((OCH,)),
             dma((QCH, 2)), dma((OCH, 2)), dma((QCH, 2)), dma((OCH, 2)),
             dma((QCH, 4)), dma((OCH, 4)), dma((QCH, 4)), dma((OCH, 4)),

time: 135 us -> 126 us (0.933)
  Pallas kernels: 132 us -> 123 us
    pallas_call x1, Pallas kernels: 131 us -> 122 us  [local(): pl.pallas_call(kernel, out_shape=(jax.ShapeDtypeStruct((192, 1152), BF16)...]
where the time goes in v3:
time: 126 us; the launch traced here: 125 us
  Pallas kernels  123 us (98%)
  local copies, waits for them, and re-layouts  2 us (2%)
    pallas_call x1, Pallas kernels, local(): pl.pallas_call(kernel, out_shape=(jax.ShapeDtypeStruct((192, 1152), BF16)...  122 us

profile of v3, /device:TPU:1, one launch (start us, length us, event | category | flops | bytes accessed | tf_op | source)
XLA Modules:
  0.0 125.5 jit_solution(14486120342655643247)
XLA Ops:
  0.6 121.9 %project.1 = (bf16[192,1152]{1,0:T(8,128)(2,1)}, bf16[192,1024]{1,0:T(8,128)(2,1)}) custom-call(bf16[96,2048]{1,0:T(8,128)(2,1)} %rows_q.1, bf16[96,2048]{1,0:T(8,128)(2,1)} %rows_o.1, bf16[128,18432]{1,0:T(8,128)(2,1)} %val_q.1, bf16[128,16384]{1,0:T(8,128)(2,1)} %val_o.1, bf16[1,144]{1,0:T(2,128)(2,1)} %scale_q.1, bf16[1,128]{1,0:T(2,128)(2,1)} %scale_o.1), custom_call_target="tpu_custom_call" | custom-call | flops 13690000384 | bytes 20000000 | tf_op jit(solution)/shard_map/project/pallas_call | solution.py:363
  122.5 0.0 copy-start
  122.5 1.0 copy-done
  123.5 0.0 copy-start.1
  123.5 1.0 copy-done.1
  124.5 0.9 place.1
Async XLA Ops:
  122.5 1.0 copy-start
  123.5 1.0 copy-start.1

commit v4 on v3

--- a/solution.py
+++ b/solution.py
@@ -11,27 +11,34 @@
 
 QCH, QW = 9, 256
 OCH, OW = 4, 512
-SWAPPED = (("o", 1), ("q", 0), ("q", 1), ("q", 2), ("q", 4), ("q", 6),)
+SWAPPED = (("o", 2, 0), ("o", 2, 1), ("o", 3, 0), ("q", 0), ("q", 1), ("q", 2), ("q", 4), ("q", 5),)
+RELAYED = (("o", 0, 0), ("o", 1, 0), ("o", 1, 1), ("o", 2, 0), ("o", 2, 1), ("o", 3, 0), ("q", 0), ("q", 1), ("q", 2), ("q", 3), ("q", 6), ("q", 7), ("q", 8),)
 CHUNKS = tuple(("q", i) for i in range(QCH)) + tuple(("o", i) for i in range(OCH))
+UNITS = tuple(("q", i) for i in range(QCH)) + tuple(("o", i, e) for i in range(OCH) for e in range(2))
 PLACE = {}
 for _p in "qo":
     for _kind in (False, True):
-        for _i, _t in enumerate(t for t in CHUNKS if t[0] == _p and (t in SWAPPED) == _kind):
+        for _i, _t in enumerate(t for t in UNITS if t[0] == _p and (t in SWAPPED) == _kind):
             PLACE[_t] = _i
 NQS, NOS = (sum(t[0] == p for t in SWAPPED) for p in "qo")
 OPS = (
-    ("o1",), ("q1",), ("w", "o", 0), ("o2",), ("q2",), ("F", "q", 0, 1), ("F", "q", 0, 3), ("w", "q", 3),
-    ("w", "o", 3), ("F", "q", 1, 1), ("F", "q", 1, 3), ("w", "q", 7), ("w", "q", 8), ("F", "q", 0, 2),
-    ("w", "q", 5), ("w", "q", 4), ("w", "q", 1), ("F", "q", 1, 2), ("F", "o", 0, 1), ("F", "o", 0, 3),
-    ("c", "q", 3), ("c", "q", 7), ("w", "o", 2), ("w", "o", 1), ("r", "q", 3), ("c", "q", 8), ("r", "q", 7),
-    ("F", "o", 0, 2), ("k", "q", 3), ("w", "q", 0), ("c", "q", 5), ("r", "q", 8), ("c", "o", 0),
-    ("c", "o", 3), ("k", "q", 7), ("r", "q", 5), ("c", "q", 4), ("w", "q", 2), ("w", "q", 6), ("k", "q", 8),
-    ("c", "q", 1), ("c", "o", 2), ("r", "o", 0), ("c", "q", 0), ("c", "o", 1), ("f", "q", 3), ("c", "q", 2),
-    ("r", "o", 3), ("f", "q", 7), ("r", "q", 4), ("c", "q", 6), ("k", "q", 5), ("f", "q", 8), ("r", "q", 1),
-    ("r", "o", 1), ("r", "o", 2), ("r", "q", 0), ("r", "q", 2), ("k", "o", 1), ("k", "o", 0), ("k", "q", 4),
-    ("k", "o", 3), ("r", "q", 6), ("k", "o", 2), ("f", "o", 0), ("f", "q", 5), ("k", "q", 1), ("f", "o", 1),
-    ("f", "o", 3), ("k", "q", 0), ("f", "q", 4), ("k", "q", 2), ("f", "q", 1), ("f", "o", 2), ("k", "q", 6),
-    ("f", "q", 0), ("f", "q", 2), ("f", "q", 6),
+    ("q1",), ("w", "o", 1), ("o1",), ("q2",), ("F", "q", 0, 1), ("F", "q", 0, 3), ("w", "q", 7), ("o2",),
+    ("F", "q", 1, 1), ("F", "q", 1, 3), ("F", "q", 0, 2), ("w", "o", 2), ("w", "q", 3), ("w", "q", 1),
+    ("F", "q", 1, 2), ("F", "o", 0, 1), ("F", "o", 0, 3), ("c", "q", 7), ("w", "q", 6), ("w", "q", 2),
+    ("w", "o", 0), ("w", "q", 0), ("w", "o", 3), ("w", "q", 4), ("w", "q", 8), ("w", "q", 5), ("c", "q", 3),
+    ("r", "q", 7), ("c", "q", 1), ("r", "q", 3), ("F", "o", 0, 2), ("c", "q", 6), ("k", "q", 7),
+    ("c", "o", 1), ("k", "q", 3), ("c", "o", 2), ("c", "q", 2), ("r", "q", 6), ("c", "o", 0), ("c", "q", 0),
+    ("r", "o", 1, 1), ("r", "o", 1, 0), ("c", "q", 4), ("k", "q", 6), ("c", "o", 3), ("c", "q", 8),
+    ("r", "q", 1), ("r", "o", 0, 1), ("s", "q", 7), ("r", "o", 0, 0), ("s", "q", 3), ("r", "q", 2),
+    ("k", "o", 1, 1), ("c", "q", 5), ("k", "o", 1, 0), ("r", "o", 2, 1), ("r", "q", 0), ("r", "o", 3, 1),
+    ("r", "o", 2, 0), ("r", "q", 4), ("r", "q", 8), ("s", "q", 6), ("r", "o", 3, 0), ("k", "o", 0, 1),
+    ("k", "q", 1), ("s", "o", 1, 1), ("f", "q", 7), ("f", "q", 3), ("k", "o", 0, 0), ("s", "o", 1, 0),
+    ("k", "q", 2), ("k", "o", 3, 1), ("k", "o", 2, 1), ("r", "q", 5), ("k", "q", 8), ("s", "q", 1),
+    ("k", "o", 2, 0), ("s", "q", 2), ("s", "o", 2, 1), ("k", "o", 3, 0), ("f", "q", 1), ("k", "q", 0),
+    ("s", "o", 2, 0), ("f", "o", 0, 1), ("f", "q", 2), ("f", "o", 1, 1), ("k", "q", 4), ("f", "o", 2, 1),
+    ("s", "o", 0, 0), ("s", "o", 3, 0), ("f", "q", 6), ("f", "o", 1, 0), ("s", "q", 0), ("k", "q", 5),
+    ("f", "o", 2, 0), ("s", "q", 8), ("f", "o", 3, 1), ("f", "o", 0, 0), ("f", "q", 4), ("f", "o", 3, 0),
+    ("f", "q", 0), ("f", "q", 8), ("f", "q", 5),
 )
 
 
@@ -39,9 +46,9 @@
     rows_q, rows_o, val_q, val_o, scale_q, scale_o,
     out_q, out_o,
     in_q, in_o, x_q, x_o, a_q, a_o, snd_q, snd_o, w_q, w_o, p_q, p_o,
-    far_q, far_o, far_qs, far_os, rx_q, rx_o, rx_qs, rx_os, ph_q, ph_o, swap, scf_q, scf_o, sc_q, sc_o,
+    far_q, far_o, far_qs, far_os, rx_q, rx_o, rx_qs, rx_os, ph_q, ph_o, swap, o_q, o_o, scf_q, scf_o, sc_q, sc_o,
     ld, s1s, s1q, s1o, s2s, s2r,
-    wsq, wso, wrq, wro, fsq, fso, frq, fro, rsq, rso, rrq, rro, psq, pso, prq, pro, sws, swr,
+    wsq, wso, wrq, wro, fsq, fso, frq, fro, rsq, rso, rrq, rro, psq, pso, prq, pro, sws, swr, outs,
 ):
     g = lax.axis_index("gx")
     w = lax.axis_index("yz")
@@ -170,6 +177,10 @@
     def rows_ready(p):
         if p not in ready:
             ready.add(p)
+            if len(ready) == 2:
+                for cp in pending:
+                    cp.wait_send()
+                pending.clear()
             for sid in range(2 if p == "q" else 1):
                 for k in range(4):
                     arrived(p, sid, piece(p, sid, 0), 4 + k)
@@ -215,18 +226,22 @@
             loads[-2 + i].wait()
         (weights_q if p == "q" else weights_o)(ch)
 
-    class Chunk:
-        def __init__(self, p, ch):
-            swapped = (p, ch) in SWAPPED
-            at = PLACE[p, ch]
-            self.p, self.ch, self.swapped = p, ch, swapped
-            self.part = p_q if p == "q" else p_o
+    class Unit:
+        def __init__(self, p, ch, e=None):
+            key = (p, ch) if p == "q" else (p, ch, e)
+            swapped = key in SWAPPED
+            at = PLACE[key]
+            self.p, self.ch, self.e, self.swapped, self.relayed = p, ch, e, swapped, key in RELAYED
             if p == "q":
                 self.far, self.rx = (far_qs, rx_qs) if swapped else (far_q, rx_q)
-                self.far_sems, self.rx_sems = (fsq, frq), (rsq, rrq)
+                self.n, self.ph = ch, ph_q.at[ch]
+                self.far_sems, self.rx_sems, self.ph_sems = (fsq, frq), (rsq, rrq), (psq, prq)
             else:
                 self.far, self.rx = (far_os, rx_os) if swapped else (far_o, rx_o)
-                self.far_sems, self.rx_sems = (fso, fro), (rso, rro)
+                self.n = 2 * ch + e
+                self.ph = ph_o.at[self.n]
+                self.rows = yh if e == 0 else 1 - yh
+                self.far_sems, self.rx_sems, self.ph_sems = (fso, fro), (rso, rro), (pso, pro)
             self.far, self.rx = self.far.at[at], self.rx.at[at]
             if not swapped:
                 self.me, self.right, self.left = x, dev(dx=1), dev(dx=3)
@@ -237,25 +252,55 @@
 
         def block(self, ahead, half):
             to = lax.rem(self.me + ahead, 4)
+            if self.p == "q":
+                if not self.swapped:
+                    return p_q.at[self.ch, half, to]
+                cols = pl.ds(pl.multiple_of(lax.rem(to, 2) * 128, 128), 128)
+                return p_q.at[self.ch, lax.div(to, 2), pl.ds(2 * half, 2), :, :, cols]
             if not self.swapped:
-                return self.part.at[self.ch, half, to]
+                return p_o.at[self.ch, self.rows, to, half]
+            cols = pl.ds(pl.multiple_of(to * 128, 128), 128)
+            return p_o.at[self.ch, self.rows, pl.ds(2 * half, 2), :, :, cols]
+
+        def last(self, ahead, half=None):
+            if self.swapped:
+                xx, yy, zz = lax.rem(x + ahead, 4), y, z
+            else:
+                xx, yy, zz = x, lax.rem(y + ahead, 4), lax.rem(z + ahead, 4)
+            i = slice(None) if half is None else half
             if self.p == "q":
-                cols = pl.ds(pl.multiple_of(lax.rem(to, 2) * 128, 128), 128)
-                return self.part.at[self.ch, lax.div(to, 2), pl.ds(2 * half, 2), :, cols]
-            cols = pl.ds(pl.multiple_of(to * 128, 128), 128)
-            return self.part.at[self.ch, half, :, :, cols]
-
-        def send_far(self, src, half, to):
-            ss, rs = self.far_sems
-            remote(src, self.far.at[half], ss.at[self.ch, half], rs.at[self.ch, half], to).start()
+                cols = pl.ds(pl.multiple_of(lax.rem(yy, 2) * 128, 128), 128)
+                return p_q.at[self.ch, lax.div(yy, 2), xx, i, :, cols]
+            return p_o.at[self.ch, self.rows, xx, i, :, pl.ds(pl.multiple_of(zz * 128, 128), 128)]
+
+        def toward(self, k):
+            return dev(dx=k) if self.swapped else dev(dy=k) if self.p == "q" else dev(dz=k)
+
+        def send(self, sems, src, dst, slot, to):
+            remote(src, dst, sems[0].at[self.n, slot], sems[1].at[self.n, slot], to).start()
+
+        def send_far(self, src, slot, to):
+            self.send(self.far_sems, src, self.far.at[slot], slot, to)
 
         def send_sum(self, src, slot, to):
-            ss, rs = self.rx_sems
-            remote(src, self.rx.at[slot], ss.at[self.ch, slot], rs.at[self.ch, slot], to).start()
+            self.send(self.rx_sems, src, self.rx.at[slot], slot, to)
+
+        def send_last(self, src, slot, sem, to):
+            self.send(self.ph_sems, src, self.ph.at[slot], sem, to)
+
+        def far_done(self, slot, way):
+            drain(self.far.at[slot], self.far_sems[way].at[self.n, slot])
+
+        def sum_done(self, slot, way):
+            drain(self.rx.at[slot], self.rx_sems[way].at[self.n, slot])
+
+        def last_done(self, slot, sem, way):
+            drain(self.ph.at[slot], self.ph_sems[way].at[self.n, sem])
+
+    SENT, CAME = 0, 1
 
     def compute(p, ch):
-        t = Chunk(p, ch)
-        a, wt, wr, wide = (a_q, w_q, wrq, QW) if p == "q" else (a_o, w_o, wro, OW)
+        a, wt, wr, part, wide = (a_q, w_q, wrq, p_q, QW) if p == "q" else (a_o, w_o, wro, p_o, OW)
         rows_ready(p)
         drain(wt.at[ch], wr.at[ch])
 
@@ -263,71 +308,94 @@
         def _(i):
             lhs = a[i].reshape(384, 1024)
             acc = jnp.dot(lhs, wt[ch], preferred_element_type=F32)
-            t.part[ch, lax.div(i, 2), pl.ds(lax.rem(i, 2) * 2, 2)] = acc.astype(BF16).reshape(2, 192, wide)
-
-        t.send_far(t.block(2, 1), 1, t.right)
-        t.send_far(t.block(2, 0), 0, t.left)
-        t.send_sum(t.block(1, 0), 0, t.right)
-        t.send_sum(t.block(3, 1), 1, t.left)
-
-    def relay(p, ch):
-        t = Chunk(p, ch)
+            part[ch, lax.div(i, 2), pl.ds(lax.rem(i, 2) * 2, 2)] = acc.astype(BF16).reshape(2, 2, 96, wide)
+
+        for t in (Unit(p, ch),) if p == "q" else (Unit(p, ch, 1), Unit(p, ch, 0)):
+            t.send_far(t.block(2, 1), 1, t.right)
+            t.send_far(t.block(2, 0), 0, t.left)
+            t.send_sum(t.block(1, 0), 0, t.right)
+            t.send_sum(t.block(3, 1), 1, t.left)
+        snd, ws = (snd_q, wsq) if p == "q" else (snd_o, wso)
+        drain(snd.at[ch, pl.ds(0, 7)], ws.at[ch])
+
+    def relay(*unit):
+        t = Unit(*unit)
         for half, ahead, slot, to in ((1, 1, 2, t.right), (0, 3, 3, t.left)):
-            drain(t.far.at[half], t.far_sems[1].at[ch, half])
+            t.far_done(half, CAME)
             own = t.block(ahead, half)
             own[...] = (own[...].astype(F32) + t.far[half].astype(F32)).astype(BF16)
             t.send_sum(own, slot, to)
 
-    def collect(p, ch):
-        t = Chunk(p, ch)
+    def collect(*unit):
+        t = Unit(*unit)
         for half, (i, j) in enumerate(((0, 3), (1, 2))):
-            drain(t.rx.at[i], t.rx_sems[1].at[ch, i])
-            drain(t.rx.at[j], t.rx_sems[1].at[ch, j])
+            t.sum_done(i, CAME)
+            t.sum_done(j, CAME)
             own = t.block(0, half)
             own[...] = (own[...].astype(F32) + t.rx[i].astype(F32) + t.rx[j].astype(F32)).astype(BF16)
-        for k in (2, 1, 3):
-            xx, yy, zz = lax.rem(x + k, 4), lax.rem(y + k, 4), lax.rem(z + k, 4)
-            if p == "q":
-                hh, ll = (yh, yl) if t.swapped else (lax.div(yy, 2), lax.rem(yy, 2))
-                src = p_q.at[ch, hh, xx if t.swapped else x, :, pl.ds(pl.multiple_of(ll * 128, 128), 128)]
-                to = dev(dx=k) if t.swapped else dev(dy=k)
-                remote(src, ph_q.at[ch, k - 1], psq.at[ch, k - 1], prq.at[ch, k - 1], to).start()
-            else:
-                cols = pl.ds(pl.multiple_of((z if t.swapped else zz) * 128, 128), 128)
-                src = p_o.at[ch, :, xx if t.swapped else x, :, cols]
-                to = dev(dx=k) if t.swapped else dev(dz=k)
-                remote(src, ph_o.at[ch, k - 1], pso.at[ch, k - 1], pro.at[ch, k - 1], to).start()
-
-    def finish(p, ch):
+        if t.relayed:
+            t.send_last(t.last(2, 1), 1, 1, t.toward(1))
+            t.send_last(t.last(2, 0), 0, 0, t.toward(3))
+            t.send_last(t.last(1, 0), 2, 2, t.toward(1))
+            t.send_last(t.last(3, 1), 3, 3, t.toward(3))
+        else:
+            for k in (2, 1, 3):
+                t.send_last(t.last(k), pl.ds(2 * (k - 1), 2), k - 1, t.toward(k))
+        for slot in range(2):
+            t.far_done(slot, SENT)
+
+    def relay_last(*unit):
+        t = Unit(*unit)
+        for half, ahead, slot in ((1, 1, 4), (0, 3, 5)):
+            t.last_done(half, half, CAME)
+            own = t.last(ahead, half)
+            own[...] = (own[...].astype(F32) + t.ph[half].astype(F32)).astype(BF16)
+            t.send_last(own, slot, slot, t.toward(ahead))
+
+    placed = []
+
+    def put(src, dst, i):
+        cp = pltpu.make_async_copy(src, dst, outs.at[i])
+        cp.start()
+        placed.append(cp)
+
+    def finish(*unit):
+        t = Unit(*unit)
+        p, ch = t.p, t.ch
+        if t.relayed:
+            terms = ((2, 5), (3, 4))
+            for slot in range(2, 6):
+                t.last_done(slot, slot, CAME)
+        else:
+            terms = ((0, 2, 4), (1, 3, 5))
+            for k in range(3):
+                t.last_done(pl.ds(2 * k, 2), k, CAME)
         if p == "q":
-            cols = pl.ds(pl.multiple_of(yl * 128, 128), 128)
-            total = p_q[ch, yh, x, :, cols].astype(F32)
-            for k in range(3):
-                drain(ph_q.at[ch, k], prq.at[ch, k])
-                total += ph_q[ch, k].astype(F32)
-            out_q[:, ch * 128:(ch + 1) * 128] = total.astype(BF16)
-        else:
-            cols = pl.ds(pl.multiple_of(z * 128, 128), 128)
-            for k in range(3):
-                drain(ph_o.at[ch, k], pro.at[ch, k])
-            give, keep = 1 - yh, yh
-            for h in (give, keep):
-                total = p_o[ch, h, x, :, cols].astype(F32)
-                for k in range(3):
-                    total += ph_o[ch, k, h].astype(F32)
-                if h is give:
-                    swap[0, ch] = total.astype(BF16)
-                    remote(swap.at[0, ch], swap.at[1, ch], sws.at[ch], swr.at[ch], dev(dy=2)).start()
-                else:
-                    out_o[:, pl.ds(pl.multiple_of(yh * 512 + ch * 128, 128), 128)] = total.astype(BF16)
+            to = o_q.at[ch]
+        else:
+            to = o_o.at[ch] if t.e == 0 else swap.at[0, ch]
+        for i in range(2):
+            v = t.last(0, i)[...].astype(F32)
+            for slot in terms[i]:
+                v += t.ph[slot].astype(F32)
+            to[96 * i:96 * (i + 1)] = v.astype(BF16)
+        if p == "q":
+            put(to, out_q.at[:, ch * 128:(ch + 1) * 128], ch)
+        elif t.e == 0:
+            put(to, out_o.at[:, pl.ds(pl.multiple_of(yh * 512 + ch * 128, 128), 128)], QCH + ch)
+        else:
+            remote(swap.at[0, ch], swap.at[1, ch], sws.at[ch], swr.at[ch], dev(dy=2)).start()
+        for slot in range(4):
+            t.sum_done(slot, SENT)
 
     def settle(ch):
         drain(swap.at[1, ch], swr.at[ch])
-        out_o[:, pl.ds(pl.multiple_of((1 - yh) * 512 + ch * 128, 128), 128)] = swap[1, ch]
+        put(swap.at[1, ch], out_o.at[:, pl.ds(pl.multiple_of((1 - yh) * 512 + ch * 128, 128), 128)], QCH + OCH + ch)
 
     todo = {
         "q1": first_q, "o1": first_o, "q2": lambda: second("q"), "o2": lambda: second("o"),
-        "F": forward, "w": weights, "c": compute, "r": relay, "k": collect, "f": finish,
+        "F": forward, "w": weights, "c": compute, "r": relay, "k": collect,
+        "s": relay_last, "f": finish,
     }
     for op in OPS:
         todo[op[0]](*op[1:])
@@ -336,20 +404,18 @@
 
     for cp in pending:
         cp.wait_send()
-    for ch in range(QCH):
-        drain(snd_q.at[ch, pl.ds(0, 7)], wsq.at[ch])
     for ch in range(OCH):
-        drain(snd_o.at[ch, pl.ds(0, 7)], wso.at[ch])
         drain(swap.at[0, ch], sws.at[ch])
-    for p, ch in CHUNKS:
-        t = Chunk(p, ch)
-        for i in range(2):
-            drain(t.far.at[i], t.far_sems[0].at[ch, i])
-        for i in range(4):
-            drain(t.rx.at[i], t.rx_sems[0].at[ch, i])
-        ph, ps = (ph_q, psq) if p == "q" else (ph_o, pso)
-        for k in range(3):
-            drain(ph.at[ch, k], ps.at[ch, k])
+    for unit in UNITS:
+        t = Unit(*unit)
+        if t.relayed:
+            for slot in range(6):
+                t.last_done(slot, slot, SENT)
+        else:
+            for k in range(3):
+                t.last_done(pl.ds(2 * k, 2), k, SENT)
+    for cp in placed:
+        cp.wait()
 
 
 def place_kernel(a, b, out_a, out_b):
@@ -367,27 +433,27 @@
             jax.ShapeDtypeStruct((192, 1024), BF16),
         ),
         in_specs=[pl.BlockSpec(memory_space=pl.ANY)] * 4 + [pl.BlockSpec(memory_space=vmem)] * 2,
-        out_specs=(pl.BlockSpec(memory_space=vmem), pl.BlockSpec(memory_space=vmem)),
+        out_specs=(pl.BlockSpec(memory_space=pl.ANY), pl.BlockSpec(memory_space=pl.ANY)),
         scratch_shapes=[
             vmem((128, 18432), BF16), vmem((128, 16384), BF16),
             vmem((2, 96, 1024), BF16), vmem((4, 96, 512), BF16),
             vmem((4, 2, 2, 96, 1024), BF16), vmem((4, 2, 2, 96, 1024), BF16),
             vmem((QCH, 8, 128, QW), BF16), vmem((OCH, 8, 128, OW), BF16),
             vmem((QCH, 1024, QW), BF16), vmem((OCH, 1024, OW), BF16),
-            vmem((QCH, 2, 4, 192, QW), BF16), vmem((OCH, 2, 4, 192, OW), BF16),
-            vmem((QCH - NQS, 2, 192, QW), BF16), vmem((OCH - NOS, 2, 192, OW), BF16),
-            vmem((NQS, 2, 2, 192, 128), BF16), vmem((NOS, 2, 4, 192, 128), BF16),
-            vmem((QCH - NQS, 4, 192, QW), BF16), vmem((OCH - NOS, 4, 192, OW), BF16),
-            vmem((NQS, 4, 2, 192, 128), BF16), vmem((NOS, 4, 4, 192, 128), BF16),
-            vmem((QCH, 3, 192, 128), BF16), vmem((OCH, 3, 2, 192, 128), BF16),
-            vmem((2, OCH, 192, 128), BF16),
+            vmem((QCH, 2, 4, 2, 96, QW), BF16), vmem((OCH, 2, 4, 2, 96, OW), BF16),
+            vmem((QCH - NQS, 2, 2, 96, QW), BF16), vmem((2 * OCH - NOS, 2, 96, OW), BF16),
+            vmem((NQS, 2, 2, 2, 96, 128), BF16), vmem((NOS, 2, 2, 2, 96, 128), BF16),
+            vmem((QCH - NQS, 4, 2, 96, QW), BF16), vmem((2 * OCH - NOS, 4, 96, OW), BF16),
+            vmem((NQS, 4, 2, 2, 96, 128), BF16), vmem((NOS, 4, 2, 2, 96, 128), BF16),
+            vmem((QCH, 6, 96, 128), BF16), vmem((2 * OCH, 6, 96, 128), BF16),
+            vmem((2, OCH, 192, 128), BF16), vmem((QCH, 192, 128), BF16), vmem((OCH, 192, 128), BF16),
             vmem((1, 144), F32), vmem((1, 128), F32), pltpu.SMEM((1, 144), F32), pltpu.SMEM((1, 128), F32),
             dma((6,)), dma((4,)), dma((2,)), dma((4,)), dma((3, 8)), dma((3, 8)),
             dma((QCH,)), dma((OCH,)), dma((QCH,)), dma((OCH,)),
-            dma((QCH, 2)), dma((OCH, 2)), dma((QCH, 2)), dma((OCH, 2)),
-            dma((QCH, 4)), dma((OCH, 4)), dma((QCH, 4)), dma((OCH, 4)),
-            dma((QCH, 3)), dma((OCH, 3)), dma((QCH, 3)), dma((OCH, 3)),
-            dma((OCH,)), dma((OCH,)),
+            dma((QCH, 2)), dma((2 * OCH, 2)), dma((QCH, 2)), dma((2 * OCH, 2)),
+            dma((QCH, 4)), dma((2 * OCH, 4)), dma((QCH, 4)), dma((2 * OCH, 4)),
+            dma((QCH, 6)), dma((2 * OCH, 6)), dma((QCH, 6)), dma((2 * OCH, 6)),
+            dma((OCH,)), dma((OCH,)), dma((QCH + 2 * OCH,)),
         ],
         compiler_params=pltpu.CompilerParams(
             collective_id=0, has_side_effects=True, vmem_limit_bytes=63 * 2**20
@@ -403,7 +469,7 @@
         out_shape=tuple(jax.ShapeDtypeStruct(s.shape, BF16) for s in sums),
         in_specs=[pl.BlockSpec(memory_space=vmem)] * 2,
         out_specs=tuple([pl.BlockSpec(memory_space=vmem)] * 2),
-        compiler_params=pltpu.CompilerParams(vmem_limit_bytes=4 * 2**20),
+        compiler_params=pltpu.CompilerParams(vmem_limit_bytes=63 * 2**20),
         name="place",
     )(*sums)
 

time: 126 us -> 122 us (0.968)
  Pallas kernels: 123 us -> 121 us
  local copies, waits for them, and re-layouts: 2 us -> 0 us
    pallas_call x1, Pallas kernels: 122 us -> 119 us  [local(): pl.pallas_call(kernel, out_shape=(jax.ShapeDtypeStruct((192, 1152), BF16)...]
    unnamed x4 -> x0, local copies, waits for them, and re-layouts: 2 us -> none
where the time goes in v4:
time: 122 us
  Pallas kernels  121 us (99%)
    pallas_call x1, Pallas kernels, local(): pl.pallas_call(kernel, out_shape=(jax.ShapeDtypeStruct((192, 1152), BF16)...  119 us

profile of v4, /device:TPU:1, one launch (start us, length us, event | category | flops | bytes accessed | tf_op | source)
XLA Modules:
  0.0 121.6 jit_solution(17091147851318039331)
XLA Ops:
  0.6 118.9 %project.1 = (bf16[192,1152]{1,0:T(8,128)(2,1)}, bf16[192,1024]{1,0:T(8,128)(2,1)}) custom-call(bf16[96,2048]{1,0:T(8,128)(2,1)} %rows_q.1, bf16[96,2048]{1,0:T(8,128)(2,1)} %rows_o.1, bf16[128,18432]{1,0:T(8,128)(2,1)} %val_q.1, bf16[128,16384]{1,0:T(8,128)(2,1)} %val_o.1, bf16[1,144]{1,0:T(2,128)(2,1)} %scale_q.1, bf16[1,128]{1,0:T(2,128)(2,1)} %scale_o.1), custom_call_target="tpu_custom_call" | custom-call | flops 13690000384 | bytes 20000000 | tf_op jit(solution)/shard_map/project/pallas_call | solution.py:429
  119.5 2.1 %place.1 = (bf16[192,1152]{1,0:T(8,128)(2,1)}, bf16[192,1024]{1,0:T(8,128)(2,1)}) custom-call(bf16[192,1152]{1,0:T(8,128)(2,1)} %get-tuple-element.4.a, bf16[192,1024]{1,0:T(8,128)(2,1)} %get-tuple-element.5.b), custom_call_target="tpu_custom_call" | custom-call | tf_op jit(solution)/shard_map/place/pallas_call | solution.py:467

commit v5 on v4

--- a/solution.py
+++ b/solution.py
@@ -46,9 +46,9 @@
     rows_q, rows_o, val_q, val_o, scale_q, scale_o,
     out_q, out_o,
     in_q, in_o, x_q, x_o, a_q, a_o, snd_q, snd_o, w_q, w_o, p_q, p_o,
-    far_q, far_o, far_qs, far_os, rx_q, rx_o, rx_qs, rx_os, ph_q, ph_o, swap, o_q, o_o, scf_q, scf_o, sc_q, sc_o,
-    ld, s1s, s1q, s1o, s2s, s2r,
-    wsq, wso, wrq, wro, fsq, fso, frq, fro, rsq, rso, rrq, rro, psq, pso, prq, pro, sws, swr, outs,
+    far_q, far_o, far_qs, far_os, rx_q, rx_o, rx_qs, rx_os, ph_q, ph_o, swap, o_q, o_o, scb_q, scb_o, scf_q, scf_o, sc_q, sc_o,
+    ld, s1s, s1r, s2s, s2r,
+    ws, wrq, wro, ss, fr, rr, pr, sw, outs,
 ):
     g = lax.axis_index("gx")
     w = lax.axis_index("yz")
@@ -80,17 +80,12 @@
     for zz in range(4):
         loads.append(pltpu.make_async_copy(
             rows_o.at[:, pl.ds(zz * 512, 512)], x_o.at[zz], ld.at[1]))
+    scales = [pltpu.make_async_copy(scale_q, scb_q, ld.at[4]), pltpu.make_async_copy(scale_o, scb_o, ld.at[5])]
+    loads += scales
     loads.append(pltpu.make_async_copy(val_q, in_q, ld.at[2]))
     loads.append(pltpu.make_async_copy(val_o, in_o, ld.at[3]))
     for cp in loads:
         cp.start()
-
-    scf_q[...] = scale_q[...].astype(F32)
-    scf_o[...] = scale_o[...].astype(F32)
-    for src, dst, sem in ((scf_q, sc_q, ld.at[4]), (scf_o, sc_o, ld.at[5])):
-        cp = pltpu.make_async_copy(src, dst, sem)
-        cp.start()
-        loads.append(cp)
 
     peers = [dev(dy=dy, dz=dz) for dy in range(4) for dz in range(4) if (dy, dz) != (0, 0)]
     peers += [dev(dz=dz, dc=1) for dz in range(4)]
@@ -102,28 +97,19 @@
     pl.semaphore_wait(barrier, len(peers))
 
     own_cols = pl.ds(pl.multiple_of(yh * 512, 512), 512)
-    pending = []
-    stage = {}
 
     def first_q():
         drain(x_q, ld.at[0])
-        cp = remote(x_q.at[1 - yl], a_q.at[z, yl, c], s1s.at[0], s1q.at[0], mate)
+        cp = remote(x_q.at[1 - yl], a_q.at[z, yl, c], s1s.at[0], s1r.at[0], mate)
         cp.start()
-        here = pltpu.make_async_copy(x_q.at[yl], a_q.at[z, yl, c], s1q.at[1])
-        here.start()
-        stage["q"] = [cp], here
+        pltpu.make_async_copy(x_q.at[yl], a_q.at[z, yl, c], s1r.at[0]).start()
         stream("q", 0, x_q.at[yl])
 
     def first_o():
         drain(x_o, ld.at[1])
-        cps = []
         for k in (2, 1, 3):
-            cp = remote(x_o.at[lax.rem(z + k, 4)], a_o.at[z, yl, c, :, own_cols], s1s.at[k], s1o.at[k], dev(dz=k))
-            cp.start()
-            cps.append(cp)
-        here = pltpu.make_async_copy(x_o.at[z], a_o.at[z, yl, c, :, own_cols], s1o.at[0])
-        here.start()
-        stage["o"] = cps, here
+            remote(x_o.at[lax.rem(z + k, 4)], a_o.at[z, yl, c, :, own_cols], s1s.at[1], s1r.at[1], dev(dz=k)).start()
+        pltpu.make_async_copy(x_o.at[z], a_o.at[z, yl, c, :, own_cols], s1r.at[1]).start()
 
     def piece(p, sid, back):
         if p == "q":
@@ -139,9 +125,7 @@
 
     def push(p, sid, src, dst, slot, to):
         row = sid if p == "q" else 2
-        cp = remote(src, dst, s2s.at[row, slot], s2r.at[row, slot], to)
-        cp.start()
-        pending.append(cp)
+        remote(src, dst, s2s.at[row], s2r.at[row, slot], to).start()
 
     def arrived(p, sid, ref, slot):
         drain(ref, s2r.at[sid if p == "q" else 2, slot])
@@ -150,40 +134,30 @@
         mine = piece(p, sid, 0)
         push(p, sid, src, mine, 0, along(p, 1))
         push(p, sid, src, mine, 1, along(p, 3))
-        push(p, sid, src, mine, 4, sib)
+        push(p, sid, src, mine, 3, sib)
 
     def second(p):
-        cps, here = stage[p]
-        for cp in cps:
-            cp.wait_recv()
-        here.wait()
-        pending.extend(cps)
+        drain(x_q if p == "q" else x_o, s1r.at["qo".index(p)])
         sid = 1 if p == "q" else 0
         stream(p, sid, piece(p, sid, 0))
 
     def forward(p, sid, k):
         part = piece(p, sid, k)
         if k == 2:
-            arrived(p, sid, half(p, part, 0), 2)
-            arrived(p, sid, half(p, part, 1), 3)
+            arrived(p, sid, part, 2)
         else:
             i = k // 2
             arrived(p, sid, part, i)
-            push(p, sid, half(p, part, i), half(p, part, i), 2 + i, along(p, k))
-        push(p, sid, part, part, 4 + k, sib)
+            push(p, sid, half(p, part, i), half(p, part, i), 2, along(p, k))
+        push(p, sid, part, part, 3, sib)
 
     ready = set()
 
     def rows_ready(p):
         if p not in ready:
             ready.add(p)
-            if len(ready) == 2:
-                for cp in pending:
-                    cp.wait_send()
-                pending.clear()
             for sid in range(2 if p == "q" else 1):
-                for k in range(4):
-                    arrived(p, sid, piece(p, sid, 0), 4 + k)
+                arrived(p, sid, a_q.at[:, 0, 0] if p == "q" else a_o.at[:, 0], 3)
 
     def weights_q(ch):
         @pl.loop(0, 8)
@@ -197,7 +171,7 @@
         here = pl.ds(pl.multiple_of((z * 2 + c) * 128, 128), 128)
         for k, dc in ((2, 0), (2, 1), (1, 0), (3, 0), (1, 1), (3, 1), (0, 1)):
             slot = lax.rem(z + k, 4) * 2 + lax.rem(c + dc, 2)
-            remote(snd_q.at[ch, slot], w_q.at[ch, here], wsq.at[ch], wrq.at[ch], dev(dz=k, dc=dc)).start()
+            remote(snd_q.at[ch, slot], w_q.at[ch, here], ws.at[0], wrq.at[ch], dev(dz=k, dc=dc)).start()
         pltpu.make_async_copy(snd_q.at[ch, z * 2 + c], w_q.at[ch, here], wrq.at[ch]).start()
 
     def weights_o(ch):
@@ -213,7 +187,7 @@
         here = pl.ds(pl.multiple_of((y * 2 + c) * 128, 128), 128)
         for k, dc in ((2, 0), (2, 1), (1, 0), (3, 0), (1, 1), (3, 1), (0, 1)):
             slot = lax.rem(y + k, 4) * 2 + lax.rem(c + dc, 2)
-            remote(snd_o.at[ch, slot], w_o.at[ch, here], wso.at[ch], wro.at[ch], dev(dy=k, dc=dc)).start()
+            remote(snd_o.at[ch, slot], w_o.at[ch, here], ws.at[1], wro.at[ch], dev(dy=k, dc=dc)).start()
         pltpu.make_async_copy(snd_o.at[ch, y * 2 + c], w_o.at[ch, here], wro.at[ch]).start()
 
     loaded = set()
@@ -222,8 +196,13 @@
         if p not in loaded:
             loaded.add(p)
             i = "qo".index(p)
+            scales[i].wait()
+            wide, smem = ((scf_q, sc_q), (scf_o, sc_o))[i]
+            wide[...] = (scb_q, scb_o)[i][...].astype(F32)
+            cp = pltpu.make_async_copy(wide, smem, ld.at[4 + i])
+            cp.start()
+            cp.wait()
             drain((in_q, in_o)[i], ld.at[2 + i])
-            loads[-2 + i].wait()
         (weights_q if p == "q" else weights_o)(ch)
 
     class Unit:
@@ -235,13 +214,15 @@
             if p == "q":
                 self.far, self.rx = (far_qs, rx_qs) if swapped else (far_q, rx_q)
                 self.n, self.ph = ch, ph_q.at[ch]
-                self.far_sems, self.rx_sems, self.ph_sems = (fsq, frq), (rsq, rrq), (psq, prq)
+                self.sems = fr.at[self.n], rr.at[self.n], pr.at[self.n]
+                self.sent = ss.at[1 if swapped else 0], ss.at[5 if swapped else 4], ss.at[8]
             else:
                 self.far, self.rx = (far_os, rx_os) if swapped else (far_o, rx_o)
                 self.n = 2 * ch + e
                 self.ph = ph_o.at[self.n]
                 self.rows = yh if e == 0 else 1 - yh
-                self.far_sems, self.rx_sems, self.ph_sems = (fso, fro), (rso, rro), (pso, pro)
+                self.sems = fr.at[QCH + self.n], rr.at[QCH + self.n], pr.at[QCH + self.n]
+                self.sent = ss.at[3 if swapped else 2], ss.at[7 if swapped else 6], ss.at[9]
             self.far, self.rx = self.far.at[at], self.rx.at[at]
             if not swapped:
                 self.me, self.right, self.left = x, dev(dx=1), dev(dx=3)
@@ -276,28 +257,14 @@
         def toward(self, k):
             return dev(dx=k) if self.swapped else dev(dy=k) if self.p == "q" else dev(dz=k)
 
-        def send(self, sems, src, dst, slot, to):
-            remote(src, dst, sems[0].at[self.n, slot], sems[1].at[self.n, slot], to).start()
-
         def send_far(self, src, slot, to):
-            self.send(self.far_sems, src, self.far.at[slot], slot, to)
+            remote(src, self.far.at[slot], self.sent[0], self.sems[0], to).start()
 
         def send_sum(self, src, slot, to):
-            self.send(self.rx_sems, src, self.rx.at[slot], slot, to)
-
-        def send_last(self, src, slot, sem, to):
-            self.send(self.ph_sems, src, self.ph.at[slot], sem, to)
-
-        def far_done(self, slot, way):
-            drain(self.far.at[slot], self.far_sems[way].at[self.n, slot])
-
-        def sum_done(self, slot, way):
-            drain(self.rx.at[slot], self.rx_sems[way].at[self.n, slot])
-
-        def last_done(self, slot, sem, way):
-            drain(self.ph.at[slot], self.ph_sems[way].at[self.n, sem])
-
-    SENT, CAME = 0, 1
+            remote(src, self.rx.at[slot], self.sent[1], self.sems[1], to).start()
+
+        def send_last(self, src, slot, stage, to):
+            remote(src, self.ph.at[slot], self.sent[2], self.sems[2].at[stage], to).start()
 
     def compute(p, ch):
         a, wt, wr, part, wide = (a_q, w_q, wrq, p_q, QW) if p == "q" else (a_o, w_o, wro, p_o, OW)
@@ -315,61 +282,50 @@
             t.send_far(t.block(2, 0), 0, t.left)
             t.send_sum(t.block(1, 0), 0, t.right)
             t.send_sum(t.block(3, 1), 1, t.left)
-        snd, ws = (snd_q, wsq) if p == "q" else (snd_o, wso)
-        drain(snd.at[ch, pl.ds(0, 7)], ws.at[ch])
 
     def relay(*unit):
         t = Unit(*unit)
+        drain(t.far, t.sems[0])
         for half, ahead, slot, to in ((1, 1, 2, t.right), (0, 3, 3, t.left)):
-            t.far_done(half, CAME)
             own = t.block(ahead, half)
             own[...] = (own[...].astype(F32) + t.far[half].astype(F32)).astype(BF16)
             t.send_sum(own, slot, to)
 
     def collect(*unit):
         t = Unit(*unit)
+        drain(t.rx, t.sems[1])
         for half, (i, j) in enumerate(((0, 3), (1, 2))):
-            t.sum_done(i, CAME)
-            t.sum_done(j, CAME)
             own = t.block(0, half)
             own[...] = (own[...].astype(F32) + t.rx[i].astype(F32) + t.rx[j].astype(F32)).astype(BF16)
         if t.relayed:
-            t.send_last(t.last(2, 1), 1, 1, t.toward(1))
+            t.send_last(t.last(2, 1), 1, 0, t.toward(1))
             t.send_last(t.last(2, 0), 0, 0, t.toward(3))
-            t.send_last(t.last(1, 0), 2, 2, t.toward(1))
-            t.send_last(t.last(3, 1), 3, 3, t.toward(3))
+            t.send_last(t.last(1, 0), 2, 1, t.toward(1))
+            t.send_last(t.last(3, 1), 3, 1, t.toward(3))
         else:
             for k in (2, 1, 3):
-                t.send_last(t.last(k), pl.ds(2 * (k - 1), 2), k - 1, t.toward(k))
-        for slot in range(2):
-            t.far_done(slot, SENT)
+                t.send_last(t.last(k), pl.ds(2 * (k - 1), 2), 1, t.toward(k))
 
     def relay_last(*unit):
         t = Unit(*unit)
+        drain(t.ph.at[pl.ds(0, 2)], t.sems[2].at[0])
         for half, ahead, slot in ((1, 1, 4), (0, 3, 5)):
-            t.last_done(half, half, CAME)
             own = t.last(ahead, half)
             own[...] = (own[...].astype(F32) + t.ph[half].astype(F32)).astype(BF16)
-            t.send_last(own, slot, slot, t.toward(ahead))
-
-    placed = []
+            t.send_last(own, slot, 1, t.toward(ahead))
 
     def put(src, dst, i):
-        cp = pltpu.make_async_copy(src, dst, outs.at[i])
-        cp.start()
-        placed.append(cp)
+        pltpu.make_async_copy(src, dst, outs.at[i]).start()
 
     def finish(*unit):
         t = Unit(*unit)
         p, ch = t.p, t.ch
         if t.relayed:
             terms = ((2, 5), (3, 4))
-            for slot in range(2, 6):
-                t.last_done(slot, slot, CAME)
+            drain(t.ph.at[pl.ds(2, 4)], t.sems[2].at[1])
         else:
             terms = ((0, 2, 4), (1, 3, 5))
-            for k in range(3):
-                t.last_done(pl.ds(2 * k, 2), k, CAME)
+            drain(t.ph, t.sems[2].at[1])
         if p == "q":
             to = o_q.at[ch]
         else:
@@ -380,17 +336,11 @@
                 v += t.ph[slot].astype(F32)
             to[96 * i:96 * (i + 1)] = v.astype(BF16)
         if p == "q":
-            put(to, out_q.at[:, ch * 128:(ch + 1) * 128], ch)
+            put(to, out_q.at[:, ch * 128:(ch + 1) * 128], 0)
         elif t.e == 0:
-            put(to, out_o.at[:, pl.ds(pl.multiple_of(yh * 512 + ch * 128, 128), 128)], QCH + ch)
+            put(to, out_o.at[:, pl.ds(pl.multiple_of(yh * 512 + ch * 128, 128), 128)], 1)
         else:
-            remote(swap.at[0, ch], swap.at[1, ch], sws.at[ch], swr.at[ch], dev(dy=2)).start()
-        for slot in range(4):
-            t.sum_done(slot, SENT)
-
-    def settle(ch):
-        drain(swap.at[1, ch], swr.at[ch])
-        put(swap.at[1, ch], out_o.at[:, pl.ds(pl.multiple_of((1 - yh) * 512 + ch * 128, 128), 128)], QCH + OCH + ch)
+            remote(swap.at[0, ch], swap.at[1, ch], sw.at[0], sw.at[1], dev(dy=2)).start()
 
     todo = {
         "q1": first_q, "o1": first_o, "q2": lambda: second("q"), "o2": lambda: second("o"),
@@ -399,28 +349,37 @@
     }
     for op in OPS:
         todo[op[0]](*op[1:])
+    drain(swap.at[1], sw.at[1])
     for ch in range(OCH):
-        settle(ch)
-
-    for cp in pending:
-        cp.wait_send()
-    for ch in range(OCH):
-        drain(swap.at[0, ch], sws.at[ch])
-    for unit in UNITS:
-        t = Unit(*unit)
-        if t.relayed:
-            for slot in range(6):
-                t.last_done(slot, slot, SENT)
-        else:
-            for k in range(3):
-                t.last_done(pl.ds(2 * k, 2), k, SENT)
-    for cp in placed:
+        put(swap.at[1, ch], out_o.at[:, pl.ds(pl.multiple_of((1 - yh) * 512 + ch * 128, 128), 128)], 2)
+
+    drain(x_q.at[0], s1s.at[0])
+    drain(x_o.at[pl.ds(0, 3)], s1s.at[1])
+    for row, n in ((0, 3), (1, 3), (2, 6)):
+        drain(snd_q.at[pl.ds(0, n), pl.ds(0, 7)], s2s.at[row])
+    drain(snd_q.at[:, pl.ds(0, 7)], ws.at[0])
+    drain(snd_o.at[:, pl.ds(0, 7)], ws.at[1])
+    for i, ref in enumerate((far_q, far_qs, far_o, far_os, rx_q, rx_qs, rx_o, rx_os, ph_q, ph_o)):
+        drain(ref, ss.at[i])
+    drain(swap.at[0], sw.at[0])
+    for i, ref in enumerate((o_q, o_o, swap.at[1])):
+        drain(ref, outs.at[i])
+
+
+def place_kernel(a, b, out_a, out_b, va, vb, sems):
+    ins, outs = [], []
+    for i, (src, mid, dst) in enumerate(((a, va, out_a), (b, vb, out_b))):
+        for j in range(4):
+            rows = pl.ds(48 * j, 48)
+            ins.append(pltpu.make_async_copy(src.at[rows], mid.at[rows], sems.at[0, 4 * i + j]))
+            outs.append(pltpu.make_async_copy(mid.at[rows], dst.at[rows], sems.at[1, 4 * i + j]))
+    for cp in ins:
+        cp.start()
+    for cp, after in zip(ins, outs):
         cp.wait()
-
-
-def place_kernel(a, b, out_a, out_b):
-    out_a[...] = a[...]
-    out_b[...] = b[...]
+        after.start()
+    for cp in outs:
+        cp.wait()
 
 
 def local(decode_rows, attended, qkv_values, qkv_scales, out_values, out_scales):
@@ -432,7 +391,7 @@
             jax.ShapeDtypeStruct((192, 1152), BF16),
             jax.ShapeDtypeStruct((192, 1024), BF16),
         ),
-        in_specs=[pl.BlockSpec(memory_space=pl.ANY)] * 4 + [pl.BlockSpec(memory_space=vmem)] * 2,
+        in_specs=[pl.BlockSpec(memory_space=pl.ANY)] * 6,
         out_specs=(pl.BlockSpec(memory_space=pl.ANY), pl.BlockSpec(memory_space=pl.ANY)),
         scratch_shapes=[
             vmem((128, 18432), BF16), vmem((128, 16384), BF16),
@@ -447,13 +406,10 @@
             vmem((NQS, 4, 2, 2, 96, 128), BF16), vmem((NOS, 4, 2, 2, 96, 128), BF16),
             vmem((QCH, 6, 96, 128), BF16), vmem((2 * OCH, 6, 96, 128), BF16),
             vmem((2, OCH, 192, 128), BF16), vmem((QCH, 192, 128), BF16), vmem((OCH, 192, 128), BF16),
-            vmem((1, 144), F32), vmem((1, 128), F32), pltpu.SMEM((1, 144), F32), pltpu.SMEM((1, 128), F32),
-            dma((6,)), dma((4,)), dma((2,)), dma((4,)), dma((3, 8)), dma((3, 8)),
-            dma((QCH,)), dma((OCH,)), dma((QCH,)), dma((OCH,)),
-            dma((QCH, 2)), dma((2 * OCH, 2)), dma((QCH, 2)), dma((2 * OCH, 2)),
-            dma((QCH, 4)), dma((2 * OCH, 4)), dma((QCH, 4)), dma((2 * OCH, 4)),
-            dma((QCH, 6)), dma((2 * OCH, 6)), dma((QCH, 6)), dma((2 * OCH, 6)),
-            dma((OCH,)), dma((OCH,)), dma((QCH + 2 * OCH,)),
+            vmem((1, 144), BF16), vmem((1, 128), BF16), vmem((1, 144), F32), vmem((1, 128), F32), pltpu.SMEM((1, 144), F32), pltpu.SMEM((1, 128), F32),
+            dma((6,)), dma((2,)), dma((2,)), dma((3,)), dma((3, 4)),
+            dma((2,)), dma((QCH,)), dma((OCH,)), dma((10,)),
+            dma((len(UNITS),)), dma((len(UNITS),)), dma((len(UNITS), 2)), dma((2,)), dma((3,)),
         ],
         compiler_params=pltpu.CompilerParams(
             collective_id=0, has_side_effects=True, vmem_limit_bytes=63 * 2**20
@@ -467,8 +423,9 @@
     return pl.pallas_call(
         place_kernel,
         out_shape=tuple(jax.ShapeDtypeStruct(s.shape, BF16) for s in sums),
-        in_specs=[pl.BlockSpec(memory_space=vmem)] * 2,
-        out_specs=tuple([pl.BlockSpec(memory_space=vmem)] * 2),
+        in_specs=[pl.BlockSpec(memory_space=pl.ANY)] * 2,
+        out_specs=tuple([pl.BlockSpec(memory_space=pl.ANY)] * 2),
+        scratch_shapes=[vmem((192, 1152), BF16), vmem((192, 1024), BF16), dma((2, 8))],
         compiler_params=pltpu.CompilerParams(vmem_limit_bytes=63 * 2**20),
         name="place",
     )(*sums)

time: 122 us -> 118 us (0.967)
  Pallas kernels: 121 us -> 116 us
    pallas_call x1, Pallas kernels: 119 us -> 114 us  [local(): pl.pallas_call(kernel, out_shape=(jax.ShapeDtypeStruct((192, 1152), BF16)...]
where the time goes in v5:
time: 118 us; the launch traced here: 117 us
  Pallas kernels  116 us (98%)
    pallas_call x1, Pallas kernels, local(): pl.pallas_call(kernel, out_shape=(jax.ShapeDtypeStruct((192, 1152), BF16)...  114 us

profile of v5, /device:TPU:1, one launch (start us, length us, event | category | flops | bytes accessed | tf_op | source)
XLA Modules:
  0.0 117.1 jit_solution(17401886290581025568)
XLA Ops:
  0.6 114.5 %project.1 = (bf16[192,1152]{1,0:T(8,128)(2,1)}, bf16[192,1024]{1,0:T(8,128)(2,1)}) custom-call(bf16[96,2048]{1,0:T(8,128)(2,1)} %rows_q.1, bf16[96,2048]{1,0:T(8,128)(2,1)} %rows_o.1, bf16[128,18432]{1,0:T(8,128)(2,1)} %val_q.1, bf16[128,16384]{1,0:T(8,128)(2,1)} %val_o.1, bf16[1,144]{1,0:T(2,128)(2,1)} %scale_q.1, bf16[1,128]{1,0:T(2,128)(2,1)} %scale_o.1), custom_call_target="tpu_custom_call" | custom-call | flops 13690000384 | bytes 20000000 | tf_op jit(solution)/shard_map/project/pallas_call | solution.py:388
  115.1 2.0 %place.1 = (bf16[192,1152]{1,0:T(8,128)(2,1)}, bf16[192,1024]{1,0:T(8,128)(2,1)}) custom-call(bf16[192,1152]{1,0:T(8,128)(2,1)} %get-tuple-element.4.a, bf16[192,1024]{1,0:T(8,128)(2,1)} %get-tuple-element.5.b), custom_call_target="tpu_custom_call" | custom-call | tf_op jit(solution)/shard_map/place/pallas_call | solution.py:423

commit v6 on v5

--- a/solution.py
+++ b/solution.py
@@ -46,9 +46,9 @@
     rows_q, rows_o, val_q, val_o, scale_q, scale_o,
     out_q, out_o,
     in_q, in_o, x_q, x_o, a_q, a_o, snd_q, snd_o, w_q, w_o, p_q, p_o,
-    far_q, far_o, far_qs, far_os, rx_q, rx_o, rx_qs, rx_os, ph_q, ph_o, swap, o_q, o_o, scb_q, scb_o, scf_q, scf_o, sc_q, sc_o,
+    far_q, far_o, far_qs, far_os, rx_q, rx_o, rx_qs, rx_os, ph_q, ph_o, swap, scb_q, scb_o, scf_q, scf_o, sc_q, sc_o,
     ld, s1s, s1r, s2s, s2r,
-    ws, wrq, wro, ss, fr, rr, pr, sw, outs,
+    ws, wrq, wro, ss, fr, rr, pr, sw,
 ):
     g = lax.axis_index("gx")
     w = lax.axis_index("yz")
@@ -70,6 +70,14 @@
 
     def drain(ref, sem):
         pltpu.make_async_copy(ref, ref, sem).wait()
+
+    peers = [dev(dy=dy, dz=dz) for dy in range(4) for dz in range(4) if (dy, dz) != (0, 0)]
+    peers += [dev(dz=dz, dc=1) for dz in range(4)]
+    peers += [dev(dy=dy, dc=1) for dy in range(1, 4)]
+    peers += [dev(dx=1), dev(dx=2), dev(dx=3)]
+    barrier = pltpu.get_barrier_semaphore()
+    for peer in peers:
+        pl.semaphore_signal(barrier, inc=1, device_id=peer, device_id_type=MESH)
 
     loads = []
     for half in range(2):
@@ -87,13 +95,6 @@
     for cp in loads:
         cp.start()
 
-    peers = [dev(dy=dy, dz=dz) for dy in range(4) for dz in range(4) if (dy, dz) != (0, 0)]
-    peers += [dev(dz=dz, dc=1) for dz in range(4)]
-    peers += [dev(dy=dy, dc=1) for dy in range(1, 4)]
-    peers += [dev(dx=1), dev(dx=2), dev(dx=3)]
-    barrier = pltpu.get_barrier_semaphore()
-    for peer in peers:
-        pl.semaphore_signal(barrier, inc=1, device_id=peer, device_id_type=MESH)
     pl.semaphore_wait(barrier, len(peers))
 
     own_cols = pl.ds(pl.multiple_of(yh * 512, 512), 512)
@@ -314,9 +315,6 @@
             own[...] = (own[...].astype(F32) + t.ph[half].astype(F32)).astype(BF16)
             t.send_last(own, slot, 1, t.toward(ahead))
 
-    def put(src, dst, i):
-        pltpu.make_async_copy(src, dst, outs.at[i]).start()
-
     def finish(*unit):
         t = Unit(*unit)
         p, ch = t.p, t.ch
@@ -327,19 +325,17 @@
             terms = ((0, 2, 4), (1, 3, 5))
             drain(t.ph, t.sems[2].at[1])
         if p == "q":
-            to = o_q.at[ch]
+            to = out_q.at[:, ch * 128:(ch + 1) * 128]
+        elif t.e == 0:
+            to = out_o.at[:, pl.ds(pl.multiple_of(yh * 512 + ch * 128, 128), 128)]
         else:
-            to = o_o.at[ch] if t.e == 0 else swap.at[0, ch]
+            to = swap.at[0, ch]
         for i in range(2):
             v = t.last(0, i)[...].astype(F32)
             for slot in terms[i]:
                 v += t.ph[slot].astype(F32)
             to[96 * i:96 * (i + 1)] = v.astype(BF16)
-        if p == "q":
-            put(to, out_q.at[:, ch * 128:(ch + 1) * 128], 0)
-        elif t.e == 0:
-            put(to, out_o.at[:, pl.ds(pl.multiple_of(yh * 512 + ch * 128, 128), 128)], 1)
-        else:
+        if p == "o" and t.e == 1:
             remote(swap.at[0, ch], swap.at[1, ch], sw.at[0], sw.at[1], dev(dy=2)).start()
 
     todo = {
@@ -351,7 +347,7 @@
         todo[op[0]](*op[1:])
     drain(swap.at[1], sw.at[1])
     for ch in range(OCH):
-        put(swap.at[1, ch], out_o.at[:, pl.ds(pl.multiple_of((1 - yh) * 512 + ch * 128, 128), 128)], 2)
+        out_o[:, pl.ds(pl.multiple_of((1 - yh) * 512 + ch * 128, 128), 128)] = swap[1, ch]
 
     drain(x_q.at[0], s1s.at[0])
     drain(x_o.at[pl.ds(0, 3)], s1s.at[1])
@@ -362,24 +358,11 @@
     for i, ref in enumerate((far_q, far_qs, far_o, far_os, rx_q, rx_qs, rx_o, rx_os, ph_q, ph_o)):
         drain(ref, ss.at[i])
     drain(swap.at[0], sw.at[0])
-    for i, ref in enumerate((o_q, o_o, swap.at[1])):
-        drain(ref, outs.at[i])
-
-
-def place_kernel(a, b, out_a, out_b, va, vb, sems):
-    ins, outs = [], []
-    for i, (src, mid, dst) in enumerate(((a, va, out_a), (b, vb, out_b))):
-        for j in range(4):
-            rows = pl.ds(48 * j, 48)
-            ins.append(pltpu.make_async_copy(src.at[rows], mid.at[rows], sems.at[0, 4 * i + j]))
-            outs.append(pltpu.make_async_copy(mid.at[rows], dst.at[rows], sems.at[1, 4 * i + j]))
-    for cp in ins:
-        cp.start()
-    for cp, after in zip(ins, outs):
-        cp.wait()
-        after.start()
-    for cp in outs:
-        cp.wait()
+
+
+def place_kernel(a, b, out_a, out_b):
+    out_a[...] = a[...]
+    out_b[...] = b[...]
 
 
 def local(decode_rows, attended, qkv_values, qkv_scales, out_values, out_scales):
@@ -388,11 +371,11 @@
     sums = pl.pallas_call(
         kernel,
         out_shape=(
-            jax.ShapeDtypeStruct((192, 1152), BF16),
-            jax.ShapeDtypeStruct((192, 1024), BF16),
+            vmem((192, 1152), BF16),
+            vmem((192, 1024), BF16),
         ),
         in_specs=[pl.BlockSpec(memory_space=pl.ANY)] * 6,
-        out_specs=(pl.BlockSpec(memory_space=pl.ANY), pl.BlockSpec(memory_space=pl.ANY)),
+        out_specs=(pl.BlockSpec(memory_space=vmem), pl.BlockSpec(memory_space=vmem)),
         scratch_shapes=[
             vmem((128, 18432), BF16), vmem((128, 16384), BF16),
             vmem((2, 96, 1024), BF16), vmem((4, 96, 512), BF16),
@@ -405,14 +388,14 @@
             vmem((QCH - NQS, 4, 2, 96, QW), BF16), vmem((2 * OCH - NOS, 4, 96, OW), BF16),
             vmem((NQS, 4, 2, 2, 96, 128), BF16), vmem((NOS, 4, 2, 2, 96, 128), BF16),
             vmem((QCH, 6, 96, 128), BF16), vmem((2 * OCH, 6, 96, 128), BF16),
-            vmem((2, OCH, 192, 128), BF16), vmem((QCH, 192, 128), BF16), vmem((OCH, 192, 128), BF16),
+            vmem((2, OCH, 192, 128), BF16),
             vmem((1, 144), BF16), vmem((1, 128), BF16), vmem((1, 144), F32), vmem((1, 128), F32), pltpu.SMEM((1, 144), F32), pltpu.SMEM((1, 128), F32),
             dma((6,)), dma((2,)), dma((2,)), dma((3,)), dma((3, 4)),
             dma((2,)), dma((QCH,)), dma((OCH,)), dma((10,)),
-            dma((len(UNITS),)), dma((len(UNITS),)), dma((len(UNITS), 2)), dma((2,)), dma((3,)),
+            dma((len(UNITS),)), dma((len(UNITS),)), dma((len(UNITS), 2)), dma((2,)),
         ],
         compiler_params=pltpu.CompilerParams(
-            collective_id=0, has_side_effects=True, vmem_limit_bytes=63 * 2**20
+            collective_id=0, has_side_effects=True, vmem_limit_bytes=61 * 2**20
         ),
         cost_estimate=pl.CostEstimate(flops=13_690_000_000, bytes_accessed=20_000_000, transcendentals=0),
         name="project",
@@ -423,10 +406,9 @@
     return pl.pallas_call(
         place_kernel,
         out_shape=tuple(jax.ShapeDtypeStruct(s.shape, BF16) for s in sums),
-        in_specs=[pl.BlockSpec(memory_space=pl.ANY)] * 2,
-        out_specs=tuple([pl.BlockSpec(memory_space=pl.ANY)] * 2),
-        scratch_shapes=[vmem((192, 1152), BF16), vmem((192, 1024), BF16), dma((2, 8))],
-        compiler_params=pltpu.CompilerParams(vmem_limit_bytes=63 * 2**20),
+        in_specs=[pl.BlockSpec(memory_space=vmem)] * 2,
+        out_specs=tuple([pl.BlockSpec(memory_space=vmem)] * 2),
+        compiler_params=pltpu.CompilerParams(vmem_limit_bytes=4 * 2**20),
         name="place",
     )(*sums)
 

time: 118 us -> 116 us (0.983)
  no operation moved by 1% of the time
where the time goes in v6:
time: 116 us; the launch traced here: 115 us
  Pallas kernels  115 us (99%)
    pallas_call x1, Pallas kernels, local(): pl.pallas_call(kernel, out_shape=(vmem((192, 1152), BF16), vmem((192, 102...  114 us

profile of v6, /device:TPU:1, one launch (start us, length us, event | category | flops | bytes accessed | tf_op | source)
XLA Modules:
  0.0 115.4 jit_solution(6171624497980210407)
XLA Ops:
  0.6 113.8 %project.1 = (bf16[192,1152]{1,0:T(8,128)(2,1)S(1)}, bf16[192,1024]{1,0:T(8,128)(2,1)S(1)}) custom-call(bf16[96,2048]{1,0:T(8,128)(2,1)} %rows_q.1, bf16[96,2048]{1,0:T(8,128)(2,1)} %rows_o.1, bf16[128,18432]{1,0:T(8,128)(2,1)} %val_q.1, bf16[128,16384]{1,0:T(8,128)(2,1)} %val_o.1, bf16[1,144]{1,0:T(2,128)(2,1)} %scale_q.1, bf16[1,128]{1,0:T(2,128)(2,1)} %scale_o.1), custom_call_target="tpu_custom_call" | custom-call | flops 13690000384 | bytes 20000000 | tf_op jit(solution)/shard_map/project/pallas_call | solution.py:371
  114.5 0.9 place.1
